TPU v7x, 32 devices: a whole 2x2x4 slice. The times are simulated.
32 devices in a mesh: occ: 4 (over z), vir: 8 (over y, x, core).
Axes of the slice: x: 2, y: 2, z: 4, core: 2. Of those that a mesh axis runs over, the one named last changes fastest.
Arguments:
- amplitudes: bfloat16 [512, 6144], P('vir', 'occ'), may hold values from -6 to 6
- tiles: bfloat16 [4, 8, 48, 9216], P('occ', 'vir'), may hold values from -0.1875 to 0.1875
- tile_map: int32 [4, 8, 48], P('occ', 'vir'), may hold values from 0 to 128, as said below
Outputs:
- residual: bfloat16 [512, 6144], P('occ', 'vir')
Inputs may be any that keep to these rules, and one draw needn't show every extreme that they name: `tile_map`: in each device's list of 48 slots the live entries name distinct tile pairs and come first; the value 16 * 8 marks an empty slot; some device has all 48 slots live.
All inputs are finite; a program needn't handle non-finite values.
Results may differ from a plain program's by a relative error of at most 0.022.
Values may be sent and summed in bfloat16 or wider, within the bound.
No kernel may reach another device: no remote copies, remote signals or barrier semaphores. Data moves between devices by JAX's collectives and lax.ppermute only.
A program may use at most 64 MiB of HBM per device.

v0:
```python
import jax
import jax.numpy as jnp
from jax import lax
from jax.sharding import PartitionSpec as P

TILE = 96
CON_TILES = 16
RES_TILES = 8


def densify(tiles, tile_map):
    slot_ids = tile_map.reshape(-1)
    slot_count = slot_ids.shape[0]
    flat_tiles = tiles.reshape(slot_count, TILE * TILE)
    pair_ids = jnp.arange(CON_TILES * RES_TILES, dtype=jnp.int32)
    onehot = (slot_ids[:, None] == pair_ids[None, :]).astype(jnp.bfloat16)
    placed = jnp.einsum("sp,sq->pq", onehot, flat_tiles, preferred_element_type=jnp.float32)
    placed = placed.astype(jnp.bfloat16).reshape(CON_TILES, RES_TILES, TILE, TILE)
    return placed.transpose(0, 2, 1, 3).reshape(CON_TILES * TILE, RES_TILES * TILE)


def per_device(amplitudes, tiles, tile_map):
    integral_block = densify(tiles, tile_map)
    gathered = lax.all_gather(amplitudes, "vir", axis=0, tiled=True)
    partial_value = jnp.dot(gathered, integral_block, preferred_element_type=jnp.float32)
    summed = lax.psum_scatter(
        partial_value.astype(jnp.bfloat16), "occ", scatter_dimension=0, tiled=True
    )
    return summed


def solution(mesh):
    in_specs = (P("vir", "occ"), P("occ", "vir", None, None), P("occ", "vir", None))
    out_specs = P("occ", "vir")
    return jax.shard_map(
        per_device, mesh=mesh, in_specs=in_specs, out_specs=out_specs, check_vma=False
    )
```

profile of v0, /device:TPU:0, one launch (start us, length us, event | category | flops | bytes accessed | tf_op | source)
XLA Modules:
  0.0 74.0 jit_solution(4184626643615082204)
XLA Ops:
  6.5 0.0 copy-start
  6.5 0.0 all-gather.2.cloned.1.call-start
  6.5 0.7 all-gather.2.cloned.1.call-update
  7.3 0.0 reduce-scatter.4.cloned.1.call-start
  7.3 0.4 copy-done
  7.7 1.5 %convolution_convert_fusion = bf16[128,9216]{1,0:T(8,128)(2,1)S(1)} fusion(bf16[1,1,48,9216]{3,2,1,0:T(8,128)(2,1)S(1)} %copy-done, s32[48]{0:T(128)} %bitcast.15), kind=kOutput, calls=%fused_computation | convolution fusion | flops 114432000 | bytes 3244224 | tf_op jit(solution)/shard_map/sp,sq->pq/dot_general | solution.py:17
  9.2 4.1 %reshape.11 = bf16[16,8,96,96]{3,2,1,0:T(8,128)(2,1)} reshape(bf16[128,9216]{1,0:T(8,128)(2,1)S(1)} %convolution_convert_fusion) | data formatting | bytes 4718592 | tf_op jit(solution)/shard_map/reshape | solution.py:18
  13.4 4.9 %copy.12 = bf16[16,8,96,96]{3,1,2,0:T(8,128)(2,1)} copy(bf16[16,8,96,96]{3,2,1,0:T(8,128)(2,1)} %reshape.11) | data formatting | bytes 4718592 | tf_op jit(solution)/shard_map/reshape | solution.py:18
  18.3 5.0 %reshape.12 = bf16[1536,768]{1,0:T(8,128)(2,1)S(1)} reshape(bf16[16,96,8,96]{3,2,1,0:T(8,128)(2,1)} %bitcast.14) | data formatting | bytes 4718592 | tf_op jit(solution)/shard_map/reshape | solution.py:19
  23.3 14.4 %all-gather.2.cloned.1.call-done = bf16[512,1536]{1,0:T(8,128)(2,1)} async-done(((bf16[64,1536]{1,0:T(8,128)(2,1)}), bf16[512,1536]{1,0:T(8,128)(2,1)}) %all-gather.2.cloned.1.call-update) | async-done | bytes 1572880 | tf_op jit(solution)/shard_map/all_gather | solution.py:24
  37.7 3.7 %fusion = bf16[512,768]{0,1:T(8,128)(2,1)} fusion(bf16[1536,768]{1,0:T(8,128)(2,1)S(1)} %reshape.12, bf16[512,1536]{1,0:T(8,128)(2,1)} %all-gather.2.cloned.1.call-done), kind=kOutput, calls=%fused_computation.3 | convolution fusion | flops 1208352768 | bytes 4718592 | tf_op jit(solution)/shard_map/dot_general | solution.py:25
  41.4 2.3 %copy.9 = bf16[512,768]{1,0:T(8,128)(2,1)} copy(bf16[512,768]{0,1:T(8,128)(2,1)} %fusion) | data formatting | bytes 1572864
  43.7 0.0 reduce-scatter.4.cloned.1.call-update
  43.7 23.4 %reduce-scatter.4.cloned.1.call-done = bf16[128,768]{1,0:T(8,128)(2,1)} async-done(((bf16[512,768]{1,0:T(8,128)(2,1)}), bf16[128,768]{1,0:T(8,128)(2,1)}) %reduce-scatter.4.cloned.1.call-update) | async-done | bytes 196624 | tf_op jit(solution)/shard_map/reduce_scatter | solution.py:26
Async XLA Ops:
  6.5 1.2 %copy-start = (bf16[1,1,48,9216]{3,2,1,0:T(8,128)(2,1)S(1)}, bf16[1,1,48,9216]{3,2,1,0:T(8,128)(2,1)}, u32[]{:S(2)}) copy-start(bf16[1,1,48,9216]{3,2,1,0:T(8,128)(2,1)} %param.4) | copy-start | bytes 2654212
  6.5 31.1 %all-gather.2.cloned.1.call-start = ((), (), s32[]{:S(2)}) async-start(), calls=%async_computation.1 | async-start | bytes 1769472 | tf_op jit(solution)/shard_map/all_gather | solution.py:24
  7.3 59.9 %reduce-scatter.4.cloned.1.call-start = ((), (), s32[]{:S(2)}) async-start(), calls=%async_computation.2 | async-start | bytes 983040 | tf_op jit(solution)/shard_map/reduce_scatter | solution.py:26
Sparse Core Ops, SparseCore 0:
  9.2 28.3 all-gather.1
  43.8 23.2 reduce-scatter.3
where the time goes:
time: 74.4 us; the launch traced here: 74 us
  waiting for transfers between devices  38.6 us (52%)
  local copies, waits for them, and re-layouts  16.7 us (22%)
  between operations  13.4 us (18%)
  matrix products  5.27 us (7%)
    reduce_scatter x1, waiting for transfers between devices, per_device(): lax.psum_scatter(partial_value.astype(jnp.bfloat16), 'occ', scatter_dimen...  23.4 us
    all_gather x1, waiting for transfers between devices, per_device(): gathered = lax.all_gather(amplitudes, 'vir', axis=0, tiled=True)  14.4 us
    reshape x2, local copies, waits for them, and re-layouts, densify(): placed.astype(jnp.bfloat16).reshape(CON_TILES, RES_TILES, TILE, TILE)  9.02 us
    reshape x1, local copies, waits for them, and re-layouts, densify(): placed.transpose(0, 2, 1, 3).reshape(CON_TILES * TILE, RES_TILES * TILE)  5.01 us
    dot_general x1, matrix products, per_device(): jnp.dot(gathered, integral_block, preferred_element_type=jnp.float32)  3.73 us
    unnamed x3, local copies, waits for them, and re-layouts  2.7 us
    dot_general x1, matrix products, densify(): jnp.einsum('sp,sq->pq', onehot, flat_tiles, preferred_element_type=jnp.fl...  1.54 us
  transfers between devices with their start and end apart: 2, of which 2 were waited for; matrix products, arithmetic and copies ran while one was open for 21% of the time, Pallas kernels for 0%

commit v1 on v0

v1 whole, which is shorter than its diff:
```python
import functools

import jax
import jax.numpy as jnp
from jax import lax
from jax.experimental import pallas as pl
from jax.experimental.pallas import tpu as pltpu
from jax.sharding import PartitionSpec as P

TILE = 96
CON_TILES = 16
RES_TILES = 8
LANES = 128
PERIOD = 384
LINES = TILE * TILE // PERIOD
CON = CON_TILES * TILE
RES = RES_TILES * TILE
CUTS = (0, 64)


def densify_kernel(map_ref, tiles_ref, dense_ref, flat_ref, square_ref, slot_ref):
    slots = tiles_ref.shape[0]
    for line in range(3 * LINES):
        flat_ref[line % 3, pl.ds(line // 3, slots, stride=LINES), :] = tiles_ref[
            :, line * LANES : (line + 1) * LANES
        ].astype(jnp.float32)

    def clear(pair, carry):
        slot_ref[pair] = slots
        return carry

    lax.fori_loop(0, CON_TILES * RES_TILES + 1, clear, 0, unroll=8)
    square_ref[slots] = jnp.zeros((TILE, LANES), jnp.float32)
    lane = lax.broadcasted_iota(jnp.int32, (LINES, LANES), 1)

    def shape_slot(slot, carry):
        pair = map_ref[slot]
        slot_ref[pair] = slot
        turn = lax.rem(lax.rem(pair, RES_TILES) * TILE, LANES)
        rows = pl.ds(pl.multiple_of(slot * LINES, 8), LINES)
        x0, x1, x2 = flat_ref[0, rows, :], flat_ref[1, rows, :], flat_ref[2, rows, :]
        parts = (
            x0,
            jnp.where(lane >= 96, x0, x1),
            jnp.where(lane >= 64, x1, x2),
            x2,
        )
        for i, part in enumerate(parts):
            square_ref[slot, pl.ds(i, LINES, stride=4), :] = pltpu.roll(
                part, lax.rem(turn + 32 * i, LANES), 1
            )
        return carry

    lax.fori_loop(0, slots, shape_slot, 0, unroll=4)
    lane = lax.broadcasted_iota(jnp.int32, (TILE, LANES), 1)

    def place(con, carry):
        rows = pl.ds(pl.multiple_of(con * TILE, TILE), TILE)
        for half in range(2):
            p = [square_ref[slot_ref[con * RES_TILES + 4 * half + i]] for i in range(4)]
            out = (
                jnp.where(lane < 96, p[0], p[1]),
                jnp.where(lane < 64, p[1], p[2]),
                jnp.where(lane < 32, p[2], p[3]),
            )
            for i in range(3):
                at = (3 * half + i) * LANES
                dense_ref[rows, at : at + LANES] = out[i].astype(jnp.bfloat16)
        return carry

    lax.fori_loop(0, CON_TILES, place, 0, unroll=2)


def densify(tiles, tile_map):
    slots = tiles.shape[2]
    return pl.pallas_call(
        densify_kernel,
        out_shape=jax.ShapeDtypeStruct((CON, RES), jnp.bfloat16),
        in_specs=[
            pl.BlockSpec(memory_space=pltpu.SMEM),
            pl.BlockSpec(memory_space=pltpu.VMEM),
        ],
        out_specs=pl.BlockSpec(memory_space=pltpu.VMEM),
        scratch_shapes=[
            pltpu.VMEM((3, slots * LINES, LANES), jnp.float32),
            pltpu.VMEM((slots + 1, TILE, LANES), jnp.float32),
            pltpu.SMEM((CON_TILES * RES_TILES + 8,), jnp.int32),
        ],
        compiler_params=pltpu.CompilerParams(vmem_limit_bytes=24 * 2**20),
        cost_estimate=pl.CostEstimate(flops=6 * 10**8, bytes_accessed=8 * 10**6, transcendentals=0),
        name="densify",
    )(tile_map.reshape(slots), tiles.reshape(slots, TILE * TILE))


def ladder_kernel(chips, *refs):
    blocks, dense_ref = refs[: 2 * chips], refs[2 * chips]
    outs, rows_ref = refs[2 * chips + 1 : -1], refs[-1]
    vir = lax.axis_index("vir")
    chip, core, occ = vir // 2, lax.rem(vir, 2), lax.axis_index("occ")
    for k in range(chips):
        at = jnp.bitwise_xor(jnp.bitwise_xor(chip, k), occ)
        rows_ref[at, core] = blocks[2 * k][...]
        rows_ref[at, 1 - core] = blocks[2 * k + 1][...]
    height = rows_ref.shape[2]
    for k in range(chips):
        lhs = rows_ref[k].reshape(2 * height, CON)
        out = jnp.dot(lhs, dense_ref[...], preferred_element_type=jnp.float32)
        outs[k][...] = out.astype(jnp.bfloat16)


def ladder(blocks, dense):
    chips = len(blocks) // 2
    height = blocks[0].shape[0]
    vmem = pl.BlockSpec(memory_space=pltpu.VMEM)
    return pl.pallas_call(
        functools.partial(ladder_kernel, chips),
        out_shape=[jax.ShapeDtypeStruct((2 * height, RES), jnp.bfloat16)] * chips,
        in_specs=[vmem] * (2 * chips + 1),
        out_specs=[vmem] * chips,
        scratch_shapes=[pltpu.VMEM((chips, 2, height, CON), jnp.bfloat16)],
        compiler_params=pltpu.CompilerParams(vmem_limit_bytes=40 * 2**20),
        cost_estimate=pl.CostEstimate(
            flops=4 * chips * height * CON * RES, bytes_accessed=6 * 10**6, transcendentals=0
        ),
        name="ladder",
    )(*blocks, dense)


def swap(value, axis, size, mask):
    return lax.ppermute(value, axis, [(i, i ^ mask) for i in range(size)])


def per_device(n_occ, n_vir, amplitudes, tiles, tile_map):
    dense = densify(tiles, tile_map)
    parts = []
    for low, high in zip(CUTS, CUTS[1:]):
        mine = amplitudes[low:high]
        held = [mine] + [swap(mine, "vir", n_vir, 2 * k) for k in range(1, n_vir // 2)]
        blocks = []
        for block in held:
            blocks += [block, swap(block, "vir", n_vir, 1)]
        outs = ladder(blocks, dense)
        terms = [outs[0]] + [swap(outs[k], "occ", n_occ, k) for k in range(1, n_occ)]
        total = sum(term.astype(jnp.float32) for term in terms).astype(jnp.bfloat16)
        parts.append(total.reshape(2, high - low, RES))
    return jnp.concatenate(parts, axis=1).reshape(-1, RES)


def solution(mesh):
    in_specs = (P("vir", "occ"), P("occ", "vir", None, None), P("occ", "vir", None))
    out_specs = P("occ", "vir")
    return jax.shard_map(
        functools.partial(per_device, mesh.shape["occ"], mesh.shape["vir"]),
        mesh=mesh,
        in_specs=in_specs,
        out_specs=out_specs,
        check_vma=False,
    )
```

time: 74.4 us -> 41 us (0.55)
  the two profiles are of different devices: /device:TPU:0 before, /device:TPU:10 now
where the time goes in v1:
time: 41 us; the launch traced here: 40.8 us
  waiting for transfers between devices  26.5 us (65%)
  starting transfers between devices  7.05 us (17%)
  Pallas kernels  4.65 us (11%)
  local copies, waits for them, and re-layouts  1.83 us (4%)
  other arithmetic  0.78 us (2%)
    ppermute x10, waiting for transfers between devices, swap(): return lax.ppermute(value, axis, [(i, i ^ mask) for i in range(size)])  26.5 us
    ppermute x10, starting transfers between devices, swap(): return lax.ppermute(value, axis, [(i, i ^ mask) for i in range(size)])  7.05 us
    pallas_call x1, Pallas kernels, densify(): pl.pallas_call(densify_kernel, out_shape=jax.ShapeDtypeStruct((CON, RES),...  3.17 us
    unnamed x6, local copies, waits for them, and re-layouts  1.83 us
    pallas_call x1, Pallas kernels, ladder(): pl.pallas_call(functools.partial(ladder_kernel, chips), out_shape=[jax.Sh...  1.48 us
  transfers between devices with their start and end apart: 10, of which 6 were waited for; matrix products, arithmetic and copies ran while one was open for 0% of the time, Pallas kernels for 8%

profile of v1, /device:TPU:10, one launch (start us, length us, event | category | flops | bytes accessed | tf_op | source)
XLA Modules:
  0.0 40.8 jit_solution(16495339432269866643)
XLA Ops:
  0.0 1.5 %collective-permute-start.3 = (bf16[64,1536]{1,0:T(8,128)(2,1)}, bf16[64,1536]{1,0:T(8,128)(2,1)S(1)}, u32[]{:S(2)}, u32[]{:S(2)}) collective-permute-start(bf16[64,1536]{1,0:T(8,128)(2,1)} %refs_0_.1), channel_id=1, source_target_pairs={{0,4},{1,5},{2,6},{3,7},{4,0},{5,1},{6,2},{7,3},{8,12},{9,13},{10,... | collective-permute-start | bytes 589832 | tf_op jit(solution)/shard_map/ppermute | solution.py:130
  1.5 0.5 %collective-permute-start.1 = (bf16[64,1536]{1,0:T(8,128)(2,1)}, bf16[64,1536]{1,0:T(8,128)(2,1)S(1)}, u32[]{:S(2)}, u32[]{:S(2)}) collective-permute-start(bf16[64,1536]{1,0:T(8,128)(2,1)} %refs_0_.1), channel_id=1, source_target_pairs={{0,2},{1,3},{2,0},{3,1},{4,6},{5,7},{6,4},{7,5},{8,10},{9,11},{10,... | collective-permute-start | bytes 589832 | tf_op jit(solution)/shard_map/ppermute | solution.py:130
  2.1 1.4 %collective-permute-start.5 = (bf16[64,1536]{1,0:T(8,128)(2,1)}, bf16[64,1536]{1,0:T(8,128)(2,1)S(1)}, u32[]{:S(2)}, u32[]{:S(2)}) collective-permute-start(bf16[64,1536]{1,0:T(8,128)(2,1)} %refs_0_.1), channel_id=1, source_target_pairs={{0,6},{1,7},{2,4},{3,5},{4,2},{5,3},{6,0},{7,1},{8,14},{9,15},{10,... | collective-permute-start | bytes 589832 | tf_op jit(solution)/shard_map/ppermute | solution.py:130
  3.5 0.0 collective-permute-start
  3.5 3.6 %collective-permute-done.3.refs_4_ = bf16[64,1536]{1,0:T(8,128)(2,1)S(1)} collective-permute-done((bf16[64,1536]{1,0:T(8,128)(2,1)}, bf16[64,1536]{1,0:T(8,128)(2,1)S(1)}, u32[]{:S(2)}, u32[]{:S(2)}) %collective-permute-start.3) | collective-permute-done | bytes 196640 | tf_op jit(solution)/shard_map/ppermute | solution.py:130
  7.1 0.0 collective-permute-start.4
  7.1 2.4 %collective-permute-done.1.refs_2_ = bf16[64,1536]{1,0:T(8,128)(2,1)S(1)} collective-permute-done((bf16[64,1536]{1,0:T(8,128)(2,1)}, bf16[64,1536]{1,0:T(8,128)(2,1)S(1)}, u32[]{:S(2)}, u32[]{:S(2)}) %collective-permute-start.1) | collective-permute-done | bytes 196640 | tf_op jit(solution)/shard_map/ppermute | solution.py:130
  9.6 0.0 collective-permute-start.2
  9.6 2.7 %collective-permute-done.5.refs_6_ = bf16[64,1536]{1,0:T(8,128)(2,1)S(1)} collective-permute-done((bf16[64,1536]{1,0:T(8,128)(2,1)}, bf16[64,1536]{1,0:T(8,128)(2,1)S(1)}, u32[]{:S(2)}, u32[]{:S(2)}) %collective-permute-start.5) | collective-permute-done | bytes 196640 | tf_op jit(solution)/shard_map/ppermute | solution.py:130
  12.2 0.0 collective-permute-start.6
  12.3 1.2 %copy-done = bf16[1,1,48,9216]{3,2,1,0:T(8,128)(2,1)S(1)} copy-done((bf16[1,1,48,9216]{3,2,1,0:T(8,128)(2,1)S(1)}, bf16[1,1,48,9216]{3,2,1,0:T(8,128)(2,1)}, u32[]{:S(2)}) %copy-start) | copy-done | bytes 884760
  13.4 0.7 %copy-done.1 = s32[1,1,48]{2,1,0:T(1,128)S(1)} copy-done((s32[1,1,48]{2,1,0:T(1,128)S(1)}, s32[1,1,48]{2,1,0:T(1,128)}, u32[]{:S(2)}) %copy-start.1) | copy-done | bytes 216
  14.1 3.2 %densify.1.refs_8_ = bf16[1536,768]{1,0:T(8,128)(2,1)S(1)} custom-call(s32[48]{0:T(128)S(1)} %bitcast.3, bf16[48,9216]{1,0:T(8,128)(2,1)S(1)} %bitcast.2), custom_call_target="tpu_custom_call" | custom-call | flops 600000000 | bytes 8000000 | tf_op jit(solution)/shard_map/densify/pallas_call | solution.py:76
  17.3 0.0 collective-permute-done.refs_1_
  17.3 0.0 collective-permute-done.4.refs_5_
  17.3 0.0 collective-permute-done.2.refs_3_
  17.3 1.5 %ladder.1 = (bf16[128,768]{1,0:T(8,128)(2,1)S(1)}, bf16[128,768]{1,0:T(8,128)(2,1)S(1)}, bf16[128,768]{1,0:T(8,128)(2,1)S(1)}, bf16[128,768]{1,0:T(8,128)(2,1)S(1)}) custom-call(bf16[64,1536]{1,0:T(8,128)(2,1)S(1)} %copy-done.2, bf16[64,1536]{1,0:T(8,128)(2,1)S(1)} %collective-permute-done.refs_1_, bf16[64,1536]{1,0:T(8,128)(2,1)S(1)} %collective-permute-done.1.refs_2_, ...), custom_call_target="tpu_custom_call" | custom-call | flops 1207959552 | bytes 6000000 | tf_op jit(solution)/shard_map/ladder/pallas_call | solution.py:115
  18.8 0.5 %collective-permute-start.7 = (bf16[128,768]{1,0:T(8,128)(2,1)S(1)}, bf16[128,768]{1,0:T(8,128)(2,1)S(1)}, u32[]{:S(2)}, u32[]{:S(2)}) collective-permute-start(bf16[128,768]{1,0:T(8,128)(2,1)S(1)} %get-tuple-element.10), channel_id=1, source_target_pairs={{0,8},{8,0},{16,24},{24,16},{1,9},{9,1},{17,25},{25,17},{2,10},{10... | collective-permute-start | bytes 589832 | tf_op jit(solution)/shard_map/ppermute | solution.py:130
  19.3 2.6 %collective-permute-start.8 = (bf16[128,768]{1,0:T(8,128)(2,1)S(1)}, bf16[128,768]{1,0:T(8,128)(2,1)S(1)}, u32[]{:S(2)}, u32[]{:S(2)}) collective-permute-start(bf16[128,768]{1,0:T(8,128)(2,1)S(1)} %get-tuple-element.11), channel_id=1, source_target_pairs={{0,16},{8,24},{16,0},{24,8},{1,17},{9,25},{17,1},{25,9},{2,18},{10... | collective-permute-start | bytes 589832 | tf_op jit(solution)/shard_map/ppermute | solution.py:130
  21.9 0.5 %collective-permute-start.9 = (bf16[128,768]{1,0:T(8,128)(2,1)S(1)}, bf16[128,768]{1,0:T(8,128)(2,1)S(1)}, u32[]{:S(2)}, u32[]{:S(2)}) collective-permute-start(bf16[128,768]{1,0:T(8,128)(2,1)S(1)} %get-tuple-element.12), channel_id=1, source_target_pairs={{0,24},{8,16},{16,8},{24,0},{1,25},{9,17},{17,9},{25,1},{2,26},{10... | collective-permute-start | bytes 589832 | tf_op jit(solution)/shard_map/ppermute | solution.py:130
  22.4 5.6 %collective-permute-done.7 = bf16[128,768]{1,0:T(8,128)(2,1)S(1)} collective-permute-done((bf16[128,768]{1,0:T(8,128)(2,1)S(1)}, bf16[128,768]{1,0:T(8,128)(2,1)S(1)}, u32[]{:S(2)}, u32[]{:S(2)}) %collective-permute-start.7) | collective-permute-done | bytes 196640 | tf_op jit(solution)/shard_map/ppermute | solution.py:130
  28.0 7.7 %collective-permute-done.8 = bf16[128,768]{1,0:T(8,128)(2,1)S(1)} collective-permute-done((bf16[128,768]{1,0:T(8,128)(2,1)S(1)}, bf16[128,768]{1,0:T(8,128)(2,1)S(1)}, u32[]{:S(2)}, u32[]{:S(2)}) %collective-permute-start.8) | collective-permute-done | bytes 196640 | tf_op jit(solution)/shard_map/ppermute | solution.py:130
  35.6 4.4 %collective-permute-done.9 = bf16[128,768]{1,0:T(8,128)(2,1)S(1)} collective-permute-done((bf16[128,768]{1,0:T(8,128)(2,1)S(1)}, bf16[128,768]{1,0:T(8,128)(2,1)S(1)}, u32[]{:S(2)}, u32[]{:S(2)}) %collective-permute-start.9) | collective-permute-done | bytes 196640 | tf_op jit(solution)/shard_map/ppermute | solution.py:130
  40.1 0.8 %add_convert_fusion = bf16[128,768]{1,0:T(8,128)(2,1)} fusion(bf16[128,768]{1,0:T(8,128)(2,1)S(1)} %collective-permute-done.9, bf16[128,768]{1,0:T(8,128)(2,1)S(1)} %collective-permute-done.8, bf16[128,768]{1,0:T(8,128)(2,1)S(1)} %collective-permute-done.7, bf16[128,768]{1,0:T(8,128)(2,1)S(1)} %get-tuple-element.9), kind=kLoop, calls=%fused_computation | loop fusion | flops 786432 | bytes 983040 | tf_op jit(solution)/shard_map/convert_element_type | solution.py:144
  (5 shorter events, 0.0 us)
Async XLA Ops:
  0.0 7.1 %collective-permute-start.3 = (bf16[64,1536]{1,0:T(8,128)(2,1)}, bf16[64,1536]{1,0:T(8,128)(2,1)S(1)}, u32[]{:S(2)}, u32[]{:S(2)}) collective-permute-start(bf16[64,1536]{1,0:T(8,128)(2,1)} %refs_0_.1), channel_id=1, source_target_pairs={{0,4},{1,5},{2,6},{3,7},{4,0},{5,1},{6,2},{7,3},{8,12},{9,13},{10,... | collective-permute-start | bytes 589832 | tf_op jit(solution)/shard_map/ppermute | solution.py:130
  1.5 8.0 %collective-permute-start.1 = (bf16[64,1536]{1,0:T(8,128)(2,1)}, bf16[64,1536]{1,0:T(8,128)(2,1)S(1)}, u32[]{:S(2)}, u32[]{:S(2)}) collective-permute-start(bf16[64,1536]{1,0:T(8,128)(2,1)} %refs_0_.1), channel_id=1, source_target_pairs={{0,2},{1,3},{2,0},{3,1},{4,6},{5,7},{6,4},{7,5},{8,10},{9,11},{10,... | collective-permute-start | bytes 589832 | tf_op jit(solution)/shard_map/ppermute | solution.py:130
  2.1 10.2 %collective-permute-start.5 = (bf16[64,1536]{1,0:T(8,128)(2,1)}, bf16[64,1536]{1,0:T(8,128)(2,1)S(1)}, u32[]{:S(2)}, u32[]{:S(2)}) collective-permute-start(bf16[64,1536]{1,0:T(8,128)(2,1)} %refs_0_.1), channel_id=1, source_target_pairs={{0,6},{1,7},{2,4},{3,5},{4,2},{5,3},{6,0},{7,1},{8,14},{9,15},{10,... | collective-permute-start | bytes 589832 | tf_op jit(solution)/shard_map/ppermute | solution.py:130
  3.5 13.8 %collective-permute-start = (bf16[64,1536]{1,0:T(8,128)(2,1)}, bf16[64,1536]{1,0:T(8,128)(2,1)S(1)}, u32[]{:S(2)}, u32[]{:S(2)}) collective-permute-start(bf16[64,1536]{1,0:T(8,128)(2,1)} %refs_0_.1), channel_id=1, source_target_pairs={{0,1},{1,0},{2,3},{3,2},{4,5},{5,4},{6,7},{7,6},{8,9},{9,8},{10,11... | collective-permute-start | bytes 589832 | tf_op jit(solution)/shard_map/ppermute | solution.py:130
  7.1 10.1 %collective-permute-start.4 = (bf16[64,1536]{1,0:T(8,128)(2,1)S(1)}, bf16[64,1536]{1,0:T(8,128)(2,1)S(1)}, u32[]{:S(2)}, u32[]{:S(2)}) collective-permute-start(bf16[64,1536]{1,0:T(8,128)(2,1)S(1)} %collective-permute-done.3.refs_4_), channel_id=1, source_target_pairs={{0,1},{1,0},{2,3},{3,2},{4,5},{5,4},{6,7},{7,6},{8,9},{9,8},{10,11... | collective-permute-start | bytes 589832 | tf_op jit(solution)/shard_map/ppermute | solution.py:130
  9.6 7.7 %collective-permute-start.2 = (bf16[64,1536]{1,0:T(8,128)(2,1)S(1)}, bf16[64,1536]{1,0:T(8,128)(2,1)S(1)}, u32[]{:S(2)}, u32[]{:S(2)}) collective-permute-start(bf16[64,1536]{1,0:T(8,128)(2,1)S(1)} %collective-permute-done.1.refs_2_), channel_id=1, source_target_pairs={{0,1},{1,0},{2,3},{3,2},{4,5},{5,4},{6,7},{7,6},{8,9},{9,8},{10,11... | collective-permute-start | bytes 589832 | tf_op jit(solution)/shard_map/ppermute | solution.py:130
  12.2 5.0 %collective-permute-start.6 = (bf16[64,1536]{1,0:T(8,128)(2,1)S(1)}, bf16[64,1536]{1,0:T(8,128)(2,1)S(1)}, u32[]{:S(2)}, u32[]{:S(2)}) collective-permute-start(bf16[64,1536]{1,0:T(8,128)(2,1)S(1)} %collective-permute-done.5.refs_6_), channel_id=1, source_target_pairs={{0,1},{1,0},{2,3},{3,2},{4,5},{5,4},{6,7},{7,6},{8,9},{9,8},{10,11... | collective-permute-start | bytes 589832 | tf_op jit(solution)/shard_map/ppermute | solution.py:130
  12.3 1.2 %copy-start = (bf16[1,1,48,9216]{3,2,1,0:T(8,128)(2,1)S(1)}, bf16[1,1,48,9216]{3,2,1,0:T(8,128)(2,1)}, u32[]{:S(2)}) copy-start(bf16[1,1,48,9216]{3,2,1,0:T(8,128)(2,1)} %param.4) | copy-start | bytes 2654212
  13.4 0.7 %copy-start.1 = (s32[1,1,48]{2,1,0:T(1,128)S(1)}, s32[1,1,48]{2,1,0:T(1,128)}, u32[]{:S(2)}) copy-start(s32[1,1,48]{2,1,0:T(1,128)} %param.5) | copy-start | bytes 580
  14.1 3.2 %copy-start.2 = (bf16[64,1536]{1,0:T(8,128)(2,1)S(1)}, bf16[64,1536]{1,0:T(8,128)(2,1)}, u32[]{:S(2)}) copy-start(bf16[64,1536]{1,0:T(8,128)(2,1)} %refs_0_.1) | copy-start | bytes 589828
  18.8 9.2 %collective-permute-start.7 = (bf16[128,768]{1,0:T(8,128)(2,1)S(1)}, bf16[128,768]{1,0:T(8,128)(2,1)S(1)}, u32[]{:S(2)}, u32[]{:S(2)}) collective-permute-start(bf16[128,768]{1,0:T(8,128)(2,1)S(1)} %get-tuple-element.10), channel_id=1, source_target_pairs={{0,8},{8,0},{16,24},{24,16},{1,9},{9,1},{17,25},{25,17},{2,10},{10... | collective-permute-start | bytes 589832 | tf_op jit(solution)/shard_map/ppermute | solution.py:130
  19.3 16.3 %collective-permute-start.8 = (bf16[128,768]{1,0:T(8,128)(2,1)S(1)}, bf16[128,768]{1,0:T(8,128)(2,1)S(1)}, u32[]{:S(2)}, u32[]{:S(2)}) collective-permute-start(bf16[128,768]{1,0:T(8,128)(2,1)S(1)} %get-tuple-element.11), channel_id=1, source_target_pairs={{0,16},{8,24},{16,0},{24,8},{1,17},{9,25},{17,1},{25,9},{2,18},{10... | collective-permute-start | bytes 589832 | tf_op jit(solution)/shard_map/ppermute | solution.py:130
  21.9 18.1 %collective-permute-start.9 = (bf16[128,768]{1,0:T(8,128)(2,1)S(1)}, bf16[128,768]{1,0:T(8,128)(2,1)S(1)}, u32[]{:S(2)}, u32[]{:S(2)}) collective-permute-start(bf16[128,768]{1,0:T(8,128)(2,1)S(1)} %get-tuple-element.12), channel_id=1, source_target_pairs={{0,24},{8,16},{16,8},{24,0},{1,25},{9,17},{17,9},{25,1},{2,26},{10... | collective-permute-start | bytes 589832 | tf_op jit(solution)/shard_map/ppermute | solution.py:130

commit v2 on v1

--- a/solution.py
+++ b/solution.py
@@ -15,7 +15,6 @@
 LINES = TILE * TILE // PERIOD
 CON = CON_TILES * TILE
 RES = RES_TILES * TILE
-CUTS = (0, 64)
 
 
 def densify_kernel(map_ref, tiles_ref, dense_ref, flat_ref, square_ref, slot_ref):
@@ -93,34 +92,40 @@
 
 
 def ladder_kernel(chips, *refs):
-    blocks, dense_ref = refs[: 2 * chips], refs[2 * chips]
-    outs, rows_ref = refs[2 * chips + 1 : -1], refs[-1]
-    vir = lax.axis_index("vir")
-    chip, core, occ = vir // 2, lax.rem(vir, 2), lax.axis_index("occ")
-    for k in range(chips):
-        at = jnp.bitwise_xor(jnp.bitwise_xor(chip, k), occ)
-        rows_ref[at, core] = blocks[2 * k][...]
-        rows_ref[at, 1 - core] = blocks[2 * k + 1][...]
-    height = rows_ref.shape[2]
-    for k in range(chips):
-        lhs = rows_ref[k].reshape(2 * height, CON)
+    blocks, dense_ref = refs[:chips], refs[chips]
+    own_ref, near_ref, keep_ref, send_ref, rows_ref = refs[chips + 1 :]
+    chip, occ = lax.axis_index("vir") // 2, lax.axis_index("occ")
+    for m in range(chips):
+        rows_ref[jnp.bitwise_xor(jnp.bitwise_xor(chip, m), occ)] = blocks[m][...]
+    height = rows_ref.shape[1]
+    for k in range(0, chips, 4):
+        lhs = rows_ref[k : k + 4].reshape(4 * height, CON)
         out = jnp.dot(lhs, dense_ref[...], preferred_element_type=jnp.float32)
-        outs[k][...] = out.astype(jnp.bfloat16)
+        out = out.astype(jnp.bfloat16).reshape(4, height, RES)
+        for i in range(4):
+            if k + i == 0:
+                own_ref[...] = out[i]
+            elif k + i == 1:
+                near_ref[...] = out[i]
+            else:
+                (keep_ref, send_ref)[i % 2][(k + i) // 2 - 1] = out[i]
 
 
 def ladder(blocks, dense):
-    chips = len(blocks) // 2
+    chips = len(blocks)
     height = blocks[0].shape[0]
     vmem = pl.BlockSpec(memory_space=pltpu.VMEM)
+    one = jax.ShapeDtypeStruct((height, RES), jnp.bfloat16)
+    far = jax.ShapeDtypeStruct((chips // 2 - 1, height, RES), jnp.bfloat16)
     return pl.pallas_call(
         functools.partial(ladder_kernel, chips),
-        out_shape=[jax.ShapeDtypeStruct((2 * height, RES), jnp.bfloat16)] * chips,
-        in_specs=[vmem] * (2 * chips + 1),
-        out_specs=[vmem] * chips,
-        scratch_shapes=[pltpu.VMEM((chips, 2, height, CON), jnp.bfloat16)],
-        compiler_params=pltpu.CompilerParams(vmem_limit_bytes=40 * 2**20),
+        out_shape=[one, one, far, far],
+        in_specs=[vmem] * (chips + 1),
+        out_specs=[vmem] * 4,
+        scratch_shapes=[pltpu.VMEM((chips, height, CON), jnp.bfloat16)],
+        compiler_params=pltpu.CompilerParams(vmem_limit_bytes=32 * 2**20),
         cost_estimate=pl.CostEstimate(
-            flops=4 * chips * height * CON * RES, bytes_accessed=6 * 10**6, transcendentals=0
+            flops=2 * chips * height * CON * RES, bytes_accessed=6 * 10**6, transcendentals=0
         ),
         name="ladder",
     )(*blocks, dense)
@@ -130,20 +135,36 @@
     return lax.ppermute(value, axis, [(i, i ^ mask) for i in range(size)])
 
 
+def add(*terms):
+    return sum(term.astype(jnp.float32) for term in terms)
+
+
 def per_device(n_occ, n_vir, amplitudes, tiles, tile_map):
     dense = densify(tiles, tile_map)
-    parts = []
-    for low, high in zip(CUTS, CUTS[1:]):
-        mine = amplitudes[low:high]
-        held = [mine] + [swap(mine, "vir", n_vir, 2 * k) for k in range(1, n_vir // 2)]
-        blocks = []
-        for block in held:
-            blocks += [block, swap(block, "vir", n_vir, 1)]
-        outs = ladder(blocks, dense)
-        terms = [outs[0]] + [swap(outs[k], "occ", n_occ, k) for k in range(1, n_occ)]
-        total = sum(term.astype(jnp.float32) for term in terms).astype(jnp.bfloat16)
-        parts.append(total.reshape(2, high - low, RES))
-    return jnp.concatenate(parts, axis=1).reshape(-1, RES)
+    chips = n_vir // 2
+    held = [amplitudes] + [None] * (chips - 1)
+    for m in list(range(2, chips)) + [1]:
+        held[m] = swap(amplitudes, "vir", n_vir, 2 * m)
+    *held, dense = lax.optimization_barrier((*held, dense))
+    other = [swap(block, "vir", n_vir, 1) for block in held]
+    own, near, far = [], [], []
+    for blocks in (held, other):
+        own_part, near_part, keep, send = ladder(blocks, dense)
+        got = swap(send, "occ", n_occ, 1)
+        pair = add(keep, got).astype(jnp.bfloat16)
+        own.append(own_part)
+        near.append(near_part)
+        far.append([swap(pair[i], "occ", n_occ, 2 * i + 2) for i in range(n_occ // 2 - 1)])
+    near = swap(jnp.concatenate(near, axis=0), "occ", n_occ, 1)
+    height = own[0].shape[0]
+    near = [near[:height], near[height:]]
+    first, second = [add(own[i], near[i], *far[i]).astype(jnp.bfloat16) for i in range(2)]
+    core = lax.rem(lax.axis_index("vir"), 2)
+    return jnp.where(
+        core == 0,
+        jnp.concatenate([first, second], axis=0),
+        jnp.concatenate([second, first], axis=0),
+    )
 
 
 def solution(mesh):

time: 41 us -> 35 us (0.85)
  the two profiles are of different devices: /device:TPU:10 before, /device:TPU:0 now
where the time goes in v2:
time: 35 us; the launch traced here: 34.8 us
  waiting for transfers between devices  13.9 us (40%)
  starting transfers between devices  13.3 us (38%)
  Pallas kernels  4.78 us (14%)
  local copies, waits for them, and re-layouts  1.83 us (5%)
  other arithmetic  0.86 us (2%)
    ppermute x12, waiting for transfers between devices, swap(): return lax.ppermute(value, axis, [(i, i ^ mask) for i in range(size)])  13.9 us
    ppermute x12, starting transfers between devices, swap(): return lax.ppermute(value, axis, [(i, i ^ mask) for i in range(size)])  13.3 us
    pallas_call x1, Pallas kernels, densify(): pl.pallas_call(densify_kernel, out_shape=jax.ShapeDtypeStruct((CON, RES),...  3.17 us
    unnamed x6, local copies, waits for them, and re-layouts  1.83 us
    pallas_call x2, Pallas kernels, ladder(): pl.pallas_call(functools.partial(ladder_kernel, chips), out_shape=[one, o...  1.61 us
    select_n x1, other arithmetic, per_device(): jnp.where(core == 0, jnp.concatenate([first, second], axis=0), jnp.concat...  0.72 us
  transfers between devices with their start and end apart: 12, of which 5 were waited for; matrix products, arithmetic and copies ran while one was open for 0% of the time, Pallas kernels for 11%

profile of v2, /device:TPU:0, one launch (start us, length us, event | category | flops | bytes accessed | tf_op | source)
XLA Modules:
  0.0 34.8 jit_solution(3528808872131662536)
XLA Ops:
  0.0 2.9 %collective-permute-start = (bf16[64,1536]{1,0:T(8,128)(2,1)}, bf16[64,1536]{1,0:T(8,128)(2,1)S(1)}, u32[]{:S(2)}, u32[]{:S(2)}) collective-permute-start(bf16[64,1536]{1,0:T(8,128)(2,1)} %refs_0_), channel_id=1, source_target_pairs={{0,2},{1,3},{2,0},{3,1},{4,6},{5,7},{6,4},{7,5},{8,10},{9,11},{10,... | collective-permute-start | bytes 589832 | tf_op jit(solution)/shard_map/ppermute | solution.py:135
  2.9 1.5 %collective-permute-start.1 = (bf16[64,1536]{1,0:T(8,128)(2,1)}, bf16[64,1536]{1,0:T(8,128)(2,1)S(1)}, u32[]{:S(2)}, u32[]{:S(2)}) collective-permute-start(bf16[64,1536]{1,0:T(8,128)(2,1)} %refs_0_), channel_id=1, source_target_pairs={{0,4},{1,5},{2,6},{3,7},{4,0},{5,1},{6,2},{7,3},{8,12},{9,13},{10,... | collective-permute-start | bytes 589832 | tf_op jit(solution)/shard_map/ppermute | solution.py:135
  4.5 0.0 collective-permute-start.2
  4.5 1.2 %copy-done = bf16[1,1,48,9216]{3,2,1,0:T(8,128)(2,1)S(1)} copy-done((bf16[1,1,48,9216]{3,2,1,0:T(8,128)(2,1)S(1)}, bf16[1,1,48,9216]{3,2,1,0:T(8,128)(2,1)}, u32[]{:S(2)}) %copy-start) | copy-done | bytes 884760
  5.6 0.7 %copy-done.2 = s32[1,1,48]{2,1,0:T(1,128)S(1)} copy-done((s32[1,1,48]{2,1,0:T(1,128)S(1)}, s32[1,1,48]{2,1,0:T(1,128)}, u32[]{:S(2)}) %copy-start.2) | copy-done | bytes 216
  6.3 3.2 %densify.1.refs_4_ = bf16[1536,768]{1,0:T(8,128)(2,1)S(1)} custom-call(s32[48]{0:T(128)S(1)} %bitcast.7, bf16[48,9216]{1,0:T(8,128)(2,1)S(1)} %bitcast.6), custom_call_target="tpu_custom_call" | custom-call | flops 600000000 | bytes 8000000 | tf_op jit(solution)/shard_map/densify/pallas_call | solution.py:75
  9.5 0.0 collective-permute-done.refs_1_
  9.5 4.2 %collective-permute-done.1.refs_2_ = bf16[64,1536]{1,0:T(8,128)(2,1)S(1)} collective-permute-done((bf16[64,1536]{1,0:T(8,128)(2,1)}, bf16[64,1536]{1,0:T(8,128)(2,1)S(1)}, u32[]{:S(2)}, u32[]{:S(2)}) %collective-permute-start.1) | collective-permute-done | bytes 196640 | tf_op jit(solution)/shard_map/ppermute | solution.py:135
  13.7 0.0 collective-permute-done.2.refs_3_
  13.7 0.8 %ladder.2 = (bf16[64,768]{1,0:T(8,128)(2,1)S(1)}, bf16[64,768]{1,0:T(8,128)(2,1)S(1)}, bf16[1,64,768]{2,1,0:T(8,128)(2,1)S(1)}, bf16[1,64,768]{2,1,0:T(8,128)(2,1)S(1)}) custom-call(bf16[64,1536]{1,0:T(8,128)(2,1)S(1)} %copy-done.1, bf16[64,1536]{1,0:T(8,128)(2,1)S(1)} %collective-permute-done.refs_1_, bf16[64,1536]{1,0:T(8,128)(2,1)S(1)} %collective-permute-done.1.refs_2_, ...), custom_call_target="tpu_custom_call" | custom-call | flops 603979776 | bytes 6000000 | tf_op jit(solution)/shard_map/ladder/pallas_call | solution.py:120
  14.5 1.6 %collective-permute-start.8 = (bf16[1,64,768]{2,1,0:T(8,128)(2,1)S(1)}, bf16[1,64,768]{2,1,0:T(8,128)(2,1)S(1)}, u32[]{:S(2)}, u32[]{:S(2)}) collective-permute-start(bf16[1,64,768]{2,1,0:T(8,128)(2,1)S(1)} %get-tuple-element.27), channel_id=1, source_target_pairs={{0,8},{8,0},{16,24},{24,16},{1,9},{9,1},{17,25},{25,17},{2,10},{10... | collective-permute-start | bytes 294920 | tf_op jit(solution)/shard_map/ppermute | solution.py:135
  16.2 0.5 %collective-permute-start.4 = (bf16[64,1536]{1,0:T(8,128)(2,1)S(1)}, bf16[64,1536]{1,0:T(8,128)(2,1)S(1)}, u32[]{:S(2)}, u32[]{:S(2)}) collective-permute-start(bf16[64,1536]{1,0:T(8,128)(2,1)S(1)} %collective-permute-done.refs_1_), channel_id=1, source_target_pairs={{0,1},{1,0},{2,3},{3,2},{4,5},{5,4},{6,7},{7,6},{8,9},{9,8},{10,11... | collective-permute-start | bytes 589832 | tf_op jit(solution)/shard_map/ppermute | solution.py:135
  16.7 0.5 %collective-permute-start.6 = (bf16[64,1536]{1,0:T(8,128)(2,1)S(1)}, bf16[64,1536]{1,0:T(8,128)(2,1)S(1)}, u32[]{:S(2)}, u32[]{:S(2)}) collective-permute-start(bf16[64,1536]{1,0:T(8,128)(2,1)S(1)} %collective-permute-done.2.refs_3_), channel_id=1, source_target_pairs={{0,1},{1,0},{2,3},{3,2},{4,5},{5,4},{6,7},{7,6},{8,9},{9,8},{10,11... | collective-permute-start | bytes 589832 | tf_op jit(solution)/shard_map/ppermute | solution.py:135
  17.2 2.0 %collective-permute-done.8 = bf16[1,64,768]{2,1,0:T(8,128)(2,1)S(1)} collective-permute-done((bf16[1,64,768]{2,1,0:T(8,128)(2,1)S(1)}, bf16[1,64,768]{2,1,0:T(8,128)(2,1)S(1)}, u32[]{:S(2)}, u32[]{:S(2)}) %collective-permute-start.8) | collective-permute-done | bytes 98336 | tf_op jit(solution)/shard_map/ppermute | solution.py:135
  19.3 2.7 %collective-permute-start.9 = (bf16[64,768]{1,0:T(8,128)(2,1)S(1)}, bf16[64,768]{1,0:T(8,128)(2,1)S(1)}, u32[]{:S(2)}, u32[]{:S(2)}) collective-permute-start(bf16[64,768]{1,0:T(8,128)(2,1)S(1)} %fusion), channel_id=1, source_target_pairs={{0,16},{8,24},{16,0},{24,8},{1,17},{9,25},{17,1},{25,9},{2,18},{10... | collective-permute-start | bytes 294920 | tf_op jit(solution)/shard_map/ppermute | solution.py:135
  21.9 0.8 %ladder.3 = (bf16[64,768]{1,0:T(8,128)(2,1)S(1)}, bf16[64,768]{1,0:T(8,128)(2,1)S(1)}, bf16[1,64,768]{2,1,0:T(8,128)(2,1)S(1)}, bf16[1,64,768]{2,1,0:T(8,128)(2,1)S(1)}) custom-call(bf16[64,1536]{1,0:T(8,128)(2,1)S(1)} %collective-permute-done.3.refs_0_, bf16[64,1536]{1,0:T(8,128)(2,1)S(1)} %collective-permute-done.4.refs_1_, ...), custom_call_target="tpu_custom_call" | custom-call | flops 603979776 | bytes 6000000 | tf_op jit(solution)/shard_map/ladder/pallas_call | solution.py:120
  22.8 1.6 %collective-permute-start.10 = (bf16[1,64,768]{2,1,0:T(8,128)(2,1)S(1)}, bf16[1,64,768]{2,1,0:T(8,128)(2,1)S(1)}, u32[]{:S(2)}, u32[]{:S(2)}) collective-permute-start(bf16[1,64,768]{2,1,0:T(8,128)(2,1)S(1)} %get-tuple-element.30), channel_id=1, source_target_pairs={{0,8},{8,0},{16,24},{24,16},{1,9},{9,1},{17,25},{25,17},{2,10},{10... | collective-permute-start | bytes 294920 | tf_op jit(solution)/shard_map/ppermute | solution.py:135
  24.4 0.5 %collective-permute-start.7 = (bf16[128,768]{1,0:T(8,128)(2,1)S(1)}, bf16[128,768]{1,0:T(8,128)(2,1)S(1)}, u32[]{:S(2)}, u32[]{:S(2)}) collective-permute-start(bf16[128,768]{1,0:T(8,128)(2,1)S(1)} %pad_maximum_fusion), channel_id=1, source_target_pairs={{0,8},{8,0},{16,24},{24,16},{1,9},{9,1},{17,25},{25,17},{2,10},{10... | collective-permute-start | bytes 589832 | tf_op jit(solution)/shard_map/ppermute | solution.py:135
  24.9 3.5 %collective-permute-done.10 = bf16[1,64,768]{2,1,0:T(8,128)(2,1)S(1)} collective-permute-done((bf16[1,64,768]{2,1,0:T(8,128)(2,1)S(1)}, bf16[1,64,768]{2,1,0:T(8,128)(2,1)S(1)}, u32[]{:S(2)}, u32[]{:S(2)}) %collective-permute-start.10) | collective-permute-done | bytes 98336 | tf_op jit(solution)/shard_map/ppermute | solution.py:135
  28.4 1.4 %collective-permute-start.11 = (bf16[64,768]{1,0:T(8,128)(2,1)S(1)}, bf16[64,768]{1,0:T(8,128)(2,1)S(1)}, u32[]{:S(2)}, u32[]{:S(2)}) collective-permute-start(bf16[64,768]{1,0:T(8,128)(2,1)S(1)} %fusion.1), channel_id=1, source_target_pairs={{0,16},{8,24},{16,0},{24,8},{1,17},{9,25},{17,1},{25,9},{2,18},{10... | collective-permute-start | bytes 294920 | tf_op jit(solution)/shard_map/ppermute | solution.py:135
  29.8 1.7 %collective-permute-done.7 = bf16[128,768]{1,0:T(8,128)(2,1)S(1)} collective-permute-done((bf16[128,768]{1,0:T(8,128)(2,1)S(1)}, bf16[128,768]{1,0:T(8,128)(2,1)S(1)}, u32[]{:S(2)}, u32[]{:S(2)}) %collective-permute-start.7) | collective-permute-done | bytes 196640 | tf_op jit(solution)/shard_map/ppermute | solution.py:135
  31.5 2.5 %collective-permute-done.11 = bf16[64,768]{1,0:T(8,128)(2,1)S(1)} collective-permute-done((bf16[64,768]{1,0:T(8,128)(2,1)S(1)}, bf16[64,768]{1,0:T(8,128)(2,1)S(1)}, u32[]{:S(2)}, u32[]{:S(2)}) %collective-permute-start.11) | collective-permute-done | bytes 98336 | tf_op jit(solution)/shard_map/ppermute | solution.py:135
  34.0 0.1 add_convert_fusion.2
  34.1 0.7 %maximum_select_fusion = bf16[128,768]{1,0:T(8,128)(2,1)} fusion(bf16[64,768]{1,0:T(8,128)(2,1)S(1)} %get-tuple-element.32, bf16[64,768]{1,0:T(8,128)(2,1)S(1)} %get-tuple-element.31, pred[]{:T(512)S(6)} %eq.3), kind=kLoop, calls=%fused_computation.1 | loop fusion | flops 884736 | bytes 393217 | tf_op jit(solution)/shard_map/jit(_where)/select_n | solution.py:163
  (14 shorter events, 0.1 us)
Async XLA Ops:
  0.0 9.5 %collective-permute-start = (bf16[64,1536]{1,0:T(8,128)(2,1)}, bf16[64,1536]{1,0:T(8,128)(2,1)S(1)}, u32[]{:S(2)}, u32[]{:S(2)}) collective-permute-start(bf16[64,1536]{1,0:T(8,128)(2,1)} %refs_0_), channel_id=1, source_target_pairs={{0,2},{1,3},{2,0},{3,1},{4,6},{5,7},{6,4},{7,5},{8,10},{9,11},{10,... | collective-permute-start | bytes 589832 | tf_op jit(solution)/shard_map/ppermute | solution.py:135
  2.9 10.8 %collective-permute-start.1 = (bf16[64,1536]{1,0:T(8,128)(2,1)}, bf16[64,1536]{1,0:T(8,128)(2,1)S(1)}, u32[]{:S(2)}, u32[]{:S(2)}) collective-permute-start(bf16[64,1536]{1,0:T(8,128)(2,1)} %refs_0_), channel_id=1, source_target_pairs={{0,4},{1,5},{2,6},{3,7},{4,0},{5,1},{6,2},{7,3},{8,12},{9,13},{10,... | collective-permute-start | bytes 589832 | tf_op jit(solution)/shard_map/ppermute | solution.py:135
  4.5 9.3 %collective-permute-start.2 = (bf16[64,1536]{1,0:T(8,128)(2,1)}, bf16[64,1536]{1,0:T(8,128)(2,1)S(1)}, u32[]{:S(2)}, u32[]{:S(2)}) collective-permute-start(bf16[64,1536]{1,0:T(8,128)(2,1)} %refs_0_), channel_id=1, source_target_pairs={{0,6},{1,7},{2,4},{3,5},{4,2},{5,3},{6,0},{7,1},{8,14},{9,15},{10,... | collective-permute-start | bytes 589832 | tf_op jit(solution)/shard_map/ppermute | solution.py:135
  4.5 1.2 %copy-start = (bf16[1,1,48,9216]{3,2,1,0:T(8,128)(2,1)S(1)}, bf16[1,1,48,9216]{3,2,1,0:T(8,128)(2,1)}, u32[]{:S(2)}) copy-start(bf16[1,1,48,9216]{3,2,1,0:T(8,128)(2,1)} %param.4) | copy-start | bytes 2654212
  5.6 0.7 %copy-start.2 = (s32[1,1,48]{2,1,0:T(1,128)S(1)}, s32[1,1,48]{2,1,0:T(1,128)}, u32[]{:S(2)}) copy-start(s32[1,1,48]{2,1,0:T(1,128)} %param.5) | copy-start | bytes 580
  6.3 7.4 %copy-start.1 = (bf16[64,1536]{1,0:T(8,128)(2,1)S(1)}, bf16[64,1536]{1,0:T(8,128)(2,1)}, u32[]{:S(2)}) copy-start(bf16[64,1536]{1,0:T(8,128)(2,1)} %refs_0_) | copy-start | bytes 589828
  14.5 4.7 %collective-permute-start.8 = (bf16[1,64,768]{2,1,0:T(8,128)(2,1)S(1)}, bf16[1,64,768]{2,1,0:T(8,128)(2,1)S(1)}, u32[]{:S(2)}, u32[]{:S(2)}) collective-permute-start(bf16[1,64,768]{2,1,0:T(8,128)(2,1)S(1)} %get-tuple-element.27), channel_id=1, source_target_pairs={{0,8},{8,0},{16,24},{24,16},{1,9},{9,1},{17,25},{25,17},{2,10},{10... | collective-permute-start | bytes 294920 | tf_op jit(solution)/shard_map/ppermute | solution.py:135
  16.2 5.7 %collective-permute-start.3 = (bf16[64,1536]{1,0:T(8,128)(2,1)S(1)}, bf16[64,1536]{1,0:T(8,128)(2,1)S(1)}, u32[]{:S(2)}, u32[]{:S(2)}) collective-permute-start(bf16[64,1536]{1,0:T(8,128)(2,1)S(1)} %copy-done.1), channel_id=1, source_target_pairs={{0,1},{1,0},{2,3},{3,2},{4,5},{5,4},{6,7},{7,6},{8,9},{9,8},{10,11... | collective-permute-start | bytes 589832 | tf_op jit(solution)/shard_map/ppermute | solution.py:135
  16.2 5.7 %collective-permute-start.4 = (bf16[64,1536]{1,0:T(8,128)(2,1)S(1)}, bf16[64,1536]{1,0:T(8,128)(2,1)S(1)}, u32[]{:S(2)}, u32[]{:S(2)}) collective-permute-start(bf16[64,1536]{1,0:T(8,128)(2,1)S(1)} %collective-permute-done.refs_1_), channel_id=1, source_target_pairs={{0,1},{1,0},{2,3},{3,2},{4,5},{5,4},{6,7},{7,6},{8,9},{9,8},{10,11... | collective-permute-start | bytes 589832 | tf_op jit(solution)/shard_map/ppermute | solution.py:135
  16.7 5.2 %collective-permute-start.5 = (bf16[64,1536]{1,0:T(8,128)(2,1)S(1)}, bf16[64,1536]{1,0:T(8,128)(2,1)S(1)}, u32[]{:S(2)}, u32[]{:S(2)}) collective-permute-start(bf16[64,1536]{1,0:T(8,128)(2,1)S(1)} %collective-permute-done.1.refs_2_), channel_id=1, source_target_pairs={{0,1},{1,0},{2,3},{3,2},{4,5},{5,4},{6,7},{7,6},{8,9},{9,8},{10,11... | collective-permute-start | bytes 589832 | tf_op jit(solution)/shard_map/ppermute | solution.py:135
  16.7 5.2 %collective-permute-start.6 = (bf16[64,1536]{1,0:T(8,128)(2,1)S(1)}, bf16[64,1536]{1,0:T(8,128)(2,1)S(1)}, u32[]{:S(2)}, u32[]{:S(2)}) collective-permute-start(bf16[64,1536]{1,0:T(8,128)(2,1)S(1)} %collective-permute-done.2.refs_3_), channel_id=1, source_target_pairs={{0,1},{1,0},{2,3},{3,2},{4,5},{5,4},{6,7},{7,6},{8,9},{9,8},{10,11... | collective-permute-start | bytes 589832 | tf_op jit(solution)/shard_map/ppermute | solution.py:135
  19.3 10.6 %collective-permute-start.9 = (bf16[64,768]{1,0:T(8,128)(2,1)S(1)}, bf16[64,768]{1,0:T(8,128)(2,1)S(1)}, u32[]{:S(2)}, u32[]{:S(2)}) collective-permute-start(bf16[64,768]{1,0:T(8,128)(2,1)S(1)} %fusion), channel_id=1, source_target_pairs={{0,16},{8,24},{16,0},{24,8},{1,17},{9,25},{17,1},{25,9},{2,18},{10... | collective-permute-start | bytes 294920 | tf_op jit(solution)/shard_map/ppermute | solution.py:135
  22.8 5.6 %collective-permute-start.10 = (bf16[1,64,768]{2,1,0:T(8,128)(2,1)S(1)}, bf16[1,64,768]{2,1,0:T(8,128)(2,1)S(1)}, u32[]{:S(2)}, u32[]{:S(2)}) collective-permute-start(bf16[1,64,768]{2,1,0:T(8,128)(2,1)S(1)} %get-tuple-element.30), channel_id=1, source_target_pairs={{0,8},{8,0},{16,24},{24,16},{1,9},{9,1},{17,25},{25,17},{2,10},{10... | collective-permute-start | bytes 294920 | tf_op jit(solution)/shard_map/ppermute | solution.py:135
  24.4 7.1 %collective-permute-start.7 = (bf16[128,768]{1,0:T(8,128)(2,1)S(1)}, bf16[128,768]{1,0:T(8,128)(2,1)S(1)}, u32[]{:S(2)}, u32[]{:S(2)}) collective-permute-start(bf16[128,768]{1,0:T(8,128)(2,1)S(1)} %pad_maximum_fusion), channel_id=1, source_target_pairs={{0,8},{8,0},{16,24},{24,16},{1,9},{9,1},{17,25},{25,17},{2,10},{10... | collective-permute-start | bytes 589832 | tf_op jit(solution)/shard_map/ppermute | solution.py:135
  28.4 5.6 %collective-permute-start.11 = (bf16[64,768]{1,0:T(8,128)(2,1)S(1)}, bf16[64,768]{1,0:T(8,128)(2,1)S(1)}, u32[]{:S(2)}, u32[]{:S(2)}) collective-permute-start(bf16[64,768]{1,0:T(8,128)(2,1)S(1)} %fusion.1), channel_id=1, source_target_pairs={{0,16},{8,24},{16,0},{24,8},{1,17},{9,25},{17,1},{25,9},{2,18},{10... | collective-permute-start | bytes 294920 | tf_op jit(solution)/shard_map/ppermute | solution.py:135

commit v3 on v2

--- a/solution.py
+++ b/solution.py
@@ -147,11 +147,12 @@
         held[m] = swap(amplitudes, "vir", n_vir, 2 * m)
     *held, dense = lax.optimization_barrier((*held, dense))
     other = [swap(block, "vir", n_vir, 1) for block in held]
+    parts = [ladder(blocks, dense) for blocks in (held, other)]
+    got = [swap(send, "occ", n_occ, 1) for _, _, _, send in parts]
+    got[0], parts[1] = lax.optimization_barrier((got[0], parts[1]))
     own, near, far = [], [], []
-    for blocks in (held, other):
-        own_part, near_part, keep, send = ladder(blocks, dense)
-        got = swap(send, "occ", n_occ, 1)
-        pair = add(keep, got).astype(jnp.bfloat16)
+    for (own_part, near_part, keep, _), received in zip(parts, got):
+        pair = add(keep, received).astype(jnp.bfloat16)
         own.append(own_part)
         near.append(near_part)
         far.append([swap(pair[i], "occ", n_occ, 2 * i + 2) for i in range(n_occ // 2 - 1)])

time: 35 us -> 33 us (0.943)
  waiting for transfers between devices: 13.9 us -> 12.2 us
    ppermute x12, waiting for transfers between devices: 13.9 us -> 12.2 us  [swap(): return lax.ppermute(value, axis, [(i, i ^ mask) for i in range(size)])]
  transfers between devices with their start and end apart: 12 -> 12, of which waited for: 5 -> 4; matrix products, arithmetic and copies ran while one was open for 0% -> 0% of each run, Pallas kernels for 11% -> 15%
where the time goes in v3:
time: 33 us; the launch traced here: 32.9 us
  starting transfers between devices  13.1 us (40%)
  waiting for transfers between devices  12.2 us (37%)
  Pallas kernels  4.78 us (14%)
  local copies, waits for them, and re-layouts  1.83 us (6%)
  other arithmetic  0.86 us (3%)
    ppermute x12, starting transfers between devices, swap(): return lax.ppermute(value, axis, [(i, i ^ mask) for i in range(size)])  13.1 us
    ppermute x12, waiting for transfers between devices, swap(): return lax.ppermute(value, axis, [(i, i ^ mask) for i in range(size)])  12.2 us
    pallas_call x1, Pallas kernels, densify(): pl.pallas_call(densify_kernel, out_shape=jax.ShapeDtypeStruct((CON, RES),...  3.17 us
    unnamed x6, local copies, waits for them, and re-layouts  1.83 us
    pallas_call x2, Pallas kernels, ladder(): pl.pallas_call(functools.partial(ladder_kernel, chips), out_shape=[one, o...  1.61 us
    select_n x1, other arithmetic, per_device(): jnp.where(core == 0, jnp.concatenate([first, second], axis=0), jnp.concat...  0.72 us
  transfers between devices with their start and end apart: 12, of which 4 were waited for; matrix products, arithmetic and copies ran while one was open for 0% of the time, Pallas kernels for 15%

profile of v3, /device:TPU:0, one launch (start us, length us, event | category | flops | bytes accessed | tf_op | source)
XLA Modules:
  0.0 32.9 jit_solution(15077263029368868789)
XLA Ops:
  0.0 2.9 %collective-permute-start = (bf16[64,1536]{1,0:T(8,128)(2,1)}, bf16[64,1536]{1,0:T(8,128)(2,1)S(1)}, u32[]{:S(2)}, u32[]{:S(2)}) collective-permute-start(bf16[64,1536]{1,0:T(8,128)(2,1)} %refs_0_), channel_id=1, source_target_pairs={{0,2},{1,3},{2,0},{3,1},{4,6},{5,7},{6,4},{7,5},{8,10},{9,11},{10,... | collective-permute-start | bytes 589832 | tf_op jit(solution)/shard_map/ppermute | solution.py:135
  2.9 1.5 %collective-permute-start.1 = (bf16[64,1536]{1,0:T(8,128)(2,1)}, bf16[64,1536]{1,0:T(8,128)(2,1)S(1)}, u32[]{:S(2)}, u32[]{:S(2)}) collective-permute-start(bf16[64,1536]{1,0:T(8,128)(2,1)} %refs_0_), channel_id=1, source_target_pairs={{0,4},{1,5},{2,6},{3,7},{4,0},{5,1},{6,2},{7,3},{8,12},{9,13},{10,... | collective-permute-start | bytes 589832 | tf_op jit(solution)/shard_map/ppermute | solution.py:135
  4.5 1.2 %copy-done = bf16[1,1,48,9216]{3,2,1,0:T(8,128)(2,1)S(1)} copy-done((bf16[1,1,48,9216]{3,2,1,0:T(8,128)(2,1)S(1)}, bf16[1,1,48,9216]{3,2,1,0:T(8,128)(2,1)}, u32[]{:S(2)}) %copy-start) | copy-done | bytes 884760
  5.6 0.7 %copy-done.2 = s32[1,1,48]{2,1,0:T(1,128)S(1)} copy-done((s32[1,1,48]{2,1,0:T(1,128)S(1)}, s32[1,1,48]{2,1,0:T(1,128)}, u32[]{:S(2)}) %copy-start.2) | copy-done | bytes 216
  6.3 3.2 %densify.1.refs_4_ = bf16[1536,768]{1,0:T(8,128)(2,1)S(1)} custom-call(s32[48]{0:T(128)S(1)} %bitcast.7, bf16[48,9216]{1,0:T(8,128)(2,1)S(1)} %bitcast.6), custom_call_target="tpu_custom_call" | custom-call | flops 600000000 | bytes 8000000 | tf_op jit(solution)/shard_map/densify/pallas_call | solution.py:75
  9.5 0.0 collective-permute-done.refs_1_
  9.5 4.2 %collective-permute-done.1.refs_2_ = bf16[64,1536]{1,0:T(8,128)(2,1)S(1)} collective-permute-done((bf16[64,1536]{1,0:T(8,128)(2,1)}, bf16[64,1536]{1,0:T(8,128)(2,1)S(1)}, u32[]{:S(2)}, u32[]{:S(2)}) %collective-permute-start.1) | collective-permute-done | bytes 196640 | tf_op jit(solution)/shard_map/ppermute | solution.py:135
  13.7 0.0 collective-permute-done.2.refs_3_
  13.7 0.5 %collective-permute-start.5 = (bf16[64,1536]{1,0:T(8,128)(2,1)S(1)}, bf16[64,1536]{1,0:T(8,128)(2,1)S(1)}, u32[]{:S(2)}, u32[]{:S(2)}) collective-permute-start(bf16[64,1536]{1,0:T(8,128)(2,1)S(1)} %collective-permute-done.refs_1_), channel_id=1, source_target_pairs={{0,1},{1,0},{2,3},{3,2},{4,5},{5,4},{6,7},{7,6},{8,9},{9,8},{10,11... | collective-permute-start | bytes 589832 | tf_op jit(solution)/shard_map/ppermute | solution.py:135
  14.2 0.1 collective-permute-start.6
  14.3 0.4 %collective-permute-start.7 = (bf16[64,1536]{1,0:T(8,128)(2,1)S(1)}, bf16[64,1536]{1,0:T(8,128)(2,1)S(1)}, u32[]{:S(2)}, u32[]{:S(2)}) collective-permute-start(bf16[64,1536]{1,0:T(8,128)(2,1)S(1)} %collective-permute-done.2.refs_3_), channel_id=1, source_target_pairs={{0,1},{1,0},{2,3},{3,2},{4,5},{5,4},{6,7},{7,6},{8,9},{9,8},{10,11... | collective-permute-start | bytes 589832 | tf_op jit(solution)/shard_map/ppermute | solution.py:135
  14.8 0.8 %ladder.2 = (bf16[64,768]{1,0:T(8,128)(2,1)S(1)}, bf16[64,768]{1,0:T(8,128)(2,1)S(1)}, bf16[1,64,768]{2,1,0:T(8,128)(2,1)S(1)}, bf16[1,64,768]{2,1,0:T(8,128)(2,1)S(1)}) custom-call(bf16[64,1536]{1,0:T(8,128)(2,1)S(1)} %copy-done.1, bf16[64,1536]{1,0:T(8,128)(2,1)S(1)} %collective-permute-done.refs_1_, bf16[64,1536]{1,0:T(8,128)(2,1)S(1)} %collective-permute-done.1.refs_2_, ...), custom_call_target="tpu_custom_call" | custom-call | flops 603979776 | bytes 6000000 | tf_op jit(solution)/shard_map/ladder/pallas_call | solution.py:120
  15.6 1.6 %collective-permute-start.3 = (bf16[1,64,768]{2,1,0:T(8,128)(2,1)S(1)}, bf16[1,64,768]{2,1,0:T(8,128)(2,1)S(1)}, u32[]{:S(2)}, u32[]{:S(2)}) collective-permute-start(bf16[1,64,768]{2,1,0:T(8,128)(2,1)S(1)} %get-tuple-element.29), channel_id=1, source_target_pairs={{0,8},{8,0},{16,24},{24,16},{1,9},{9,1},{17,25},{25,17},{2,10},{10... | collective-permute-start | bytes 294920 | tf_op jit(solution)/shard_map/ppermute | solution.py:135
  17.2 0.0 collective-permute-done.4.refs_0_
  17.2 0.8 %ladder.3 = (bf16[64,768]{1,0:T(8,128)(2,1)S(1)}, bf16[64,768]{1,0:T(8,128)(2,1)S(1)}, bf16[1,64,768]{2,1,0:T(8,128)(2,1)S(1)}, bf16[1,64,768]{2,1,0:T(8,128)(2,1)S(1)}) custom-call(bf16[64,1536]{1,0:T(8,128)(2,1)S(1)} %collective-permute-done.4.refs_0_, bf16[64,1536]{1,0:T(8,128)(2,1)S(1)} %collective-permute-done.5.refs_1_, ...), custom_call_target="tpu_custom_call" | custom-call | flops 603979776 | bytes 6000000 | tf_op jit(solution)/shard_map/ladder/pallas_call | solution.py:120
  18.0 0.5 %collective-permute-start.10 = (bf16[1,64,768]{2,1,0:T(8,128)(2,1)S(1)}, bf16[1,64,768]{2,1,0:T(8,128)(2,1)S(1)}, u32[]{:S(2)}, u32[]{:S(2)}) collective-permute-start(bf16[1,64,768]{2,1,0:T(8,128)(2,1)S(1)} %get-tuple-element.33), channel_id=1, source_target_pairs={{0,8},{8,0},{16,24},{24,16},{1,9},{9,1},{17,25},{25,17},{2,10},{10... | collective-permute-start | bytes 294920 | tf_op jit(solution)/shard_map/ppermute | solution.py:135
  18.6 1.8 %collective-permute-done.3 = bf16[1,64,768]{2,1,0:T(8,128)(2,1)S(1)} collective-permute-done((bf16[1,64,768]{2,1,0:T(8,128)(2,1)S(1)}, bf16[1,64,768]{2,1,0:T(8,128)(2,1)S(1)}, u32[]{:S(2)}, u32[]{:S(2)}) %collective-permute-start.3) | collective-permute-done | bytes 98336 | tf_op jit(solution)/shard_map/ppermute | solution.py:135
  20.4 2.7 %collective-permute-start.9 = (bf16[64,768]{1,0:T(8,128)(2,1)S(1)}, bf16[64,768]{1,0:T(8,128)(2,1)S(1)}, u32[]{:S(2)}, u32[]{:S(2)}) collective-permute-start(bf16[64,768]{1,0:T(8,128)(2,1)S(1)} %fusion), channel_id=1, source_target_pairs={{0,16},{8,24},{16,0},{24,8},{1,17},{9,25},{17,1},{25,9},{2,18},{10... | collective-permute-start | bytes 294920 | tf_op jit(solution)/shard_map/ppermute | solution.py:135
  23.1 2.4 %collective-permute-start.8 = (bf16[128,768]{1,0:T(8,128)(2,1)S(1)}, bf16[128,768]{1,0:T(8,128)(2,1)S(1)}, u32[]{:S(2)}, u32[]{:S(2)}) collective-permute-start(bf16[128,768]{1,0:T(8,128)(2,1)S(1)} %pad_maximum_fusion), channel_id=1, source_target_pairs={{0,8},{8,0},{16,24},{24,16},{1,9},{9,1},{17,25},{25,17},{2,10},{10... | collective-permute-start | bytes 589832 | tf_op jit(solution)/shard_map/ppermute | solution.py:135
  25.5 0.5 %collective-permute-start.11 = (bf16[64,768]{1,0:T(8,128)(2,1)S(1)}, bf16[64,768]{1,0:T(8,128)(2,1)S(1)}, u32[]{:S(2)}, u32[]{:S(2)}) collective-permute-start(bf16[64,768]{1,0:T(8,128)(2,1)S(1)} %fusion.1), channel_id=1, source_target_pairs={{0,16},{8,24},{16,0},{24,8},{1,17},{9,25},{17,1},{25,9},{2,18},{10... | collective-permute-start | bytes 294920 | tf_op jit(solution)/shard_map/ppermute | solution.py:135
  26.0 0.8 %collective-permute-done.9 = bf16[64,768]{1,0:T(8,128)(2,1)S(1)} collective-permute-done((bf16[64,768]{1,0:T(8,128)(2,1)S(1)}, bf16[64,768]{1,0:T(8,128)(2,1)S(1)}, u32[]{:S(2)}, u32[]{:S(2)}) %collective-permute-start.9) | collective-permute-done | bytes 98336 | tf_op jit(solution)/shard_map/ppermute | solution.py:135
  26.8 5.3 %collective-permute-done.8 = bf16[128,768]{1,0:T(8,128)(2,1)S(1)} collective-permute-done((bf16[128,768]{1,0:T(8,128)(2,1)S(1)}, bf16[128,768]{1,0:T(8,128)(2,1)S(1)}, u32[]{:S(2)}, u32[]{:S(2)}) %collective-permute-start.8) | collective-permute-done | bytes 196640 | tf_op jit(solution)/shard_map/ppermute | solution.py:135
  32.1 0.1 add_convert_fusion.2
  32.2 0.7 %maximum_select_fusion = bf16[128,768]{1,0:T(8,128)(2,1)} fusion(bf16[64,768]{1,0:T(8,128)(2,1)S(1)} %get-tuple-element.40, bf16[64,768]{1,0:T(8,128)(2,1)S(1)} %get-tuple-element.39, pred[]{:T(512)S(6)} %eq.3), kind=kLoop, calls=%fused_computation.1 | loop fusion | flops 884736 | bytes 393217 | tf_op jit(solution)/shard_map/jit(_where)/select_n | solution.py:164
  (14 shorter events, 0.1 us)
Async XLA Ops:
  0.0 9.5 %collective-permute-start = (bf16[64,1536]{1,0:T(8,128)(2,1)}, bf16[64,1536]{1,0:T(8,128)(2,1)S(1)}, u32[]{:S(2)}, u32[]{:S(2)}) collective-permute-start(bf16[64,1536]{1,0:T(8,128)(2,1)} %refs_0_), channel_id=1, source_target_pairs={{0,2},{1,3},{2,0},{3,1},{4,6},{5,7},{6,4},{7,5},{8,10},{9,11},{10,... | collective-permute-start | bytes 589832 | tf_op jit(solution)/shard_map/ppermute | solution.py:135
  2.9 10.8 %collective-permute-start.1 = (bf16[64,1536]{1,0:T(8,128)(2,1)}, bf16[64,1536]{1,0:T(8,128)(2,1)S(1)}, u32[]{:S(2)}, u32[]{:S(2)}) collective-permute-start(bf16[64,1536]{1,0:T(8,128)(2,1)} %refs_0_), channel_id=1, source_target_pairs={{0,4},{1,5},{2,6},{3,7},{4,0},{5,1},{6,2},{7,3},{8,12},{9,13},{10,... | collective-permute-start | bytes 589832 | tf_op jit(solution)/shard_map/ppermute | solution.py:135
  4.5 9.3 %collective-permute-start.2 = (bf16[64,1536]{1,0:T(8,128)(2,1)}, bf16[64,1536]{1,0:T(8,128)(2,1)S(1)}, u32[]{:S(2)}, u32[]{:S(2)}) collective-permute-start(bf16[64,1536]{1,0:T(8,128)(2,1)} %refs_0_), channel_id=1, source_target_pairs={{0,6},{1,7},{2,4},{3,5},{4,2},{5,3},{6,0},{7,1},{8,14},{9,15},{10,... | collective-permute-start | bytes 589832 | tf_op jit(solution)/shard_map/ppermute | solution.py:135
  4.5 1.2 %copy-start = (bf16[1,1,48,9216]{3,2,1,0:T(8,128)(2,1)S(1)}, bf16[1,1,48,9216]{3,2,1,0:T(8,128)(2,1)}, u32[]{:S(2)}) copy-start(bf16[1,1,48,9216]{3,2,1,0:T(8,128)(2,1)} %param.4) | copy-start | bytes 2654212
  5.6 0.7 %copy-start.2 = (s32[1,1,48]{2,1,0:T(1,128)S(1)}, s32[1,1,48]{2,1,0:T(1,128)}, u32[]{:S(2)}) copy-start(s32[1,1,48]{2,1,0:T(1,128)} %param.5) | copy-start | bytes 580
  6.3 7.4 %copy-start.1 = (bf16[64,1536]{1,0:T(8,128)(2,1)S(1)}, bf16[64,1536]{1,0:T(8,128)(2,1)}, u32[]{:S(2)}) copy-start(bf16[64,1536]{1,0:T(8,128)(2,1)} %refs_0_) | copy-start | bytes 589828
  13.7 3.5 %collective-permute-start.4 = (bf16[64,1536]{1,0:T(8,128)(2,1)S(1)}, bf16[64,1536]{1,0:T(8,128)(2,1)S(1)}, u32[]{:S(2)}, u32[]{:S(2)}) collective-permute-start(bf16[64,1536]{1,0:T(8,128)(2,1)S(1)} %copy-done.1), channel_id=1, source_target_pairs={{0,1},{1,0},{2,3},{3,2},{4,5},{5,4},{6,7},{7,6},{8,9},{9,8},{10,11... | collective-permute-start | bytes 589832 | tf_op jit(solution)/shard_map/ppermute | solution.py:135
  13.7 3.5 %collective-permute-start.5 = (bf16[64,1536]{1,0:T(8,128)(2,1)S(1)}, bf16[64,1536]{1,0:T(8,128)(2,1)S(1)}, u32[]{:S(2)}, u32[]{:S(2)}) collective-permute-start(bf16[64,1536]{1,0:T(8,128)(2,1)S(1)} %collective-permute-done.refs_1_), channel_id=1, source_target_pairs={{0,1},{1,0},{2,3},{3,2},{4,5},{5,4},{6,7},{7,6},{8,9},{9,8},{10,11... | collective-permute-start | bytes 589832 | tf_op jit(solution)/shard_map/ppermute | solution.py:135
  14.2 3.0 %collective-permute-start.6 = (bf16[64,1536]{1,0:T(8,128)(2,1)S(1)}, bf16[64,1536]{1,0:T(8,128)(2,1)S(1)}, u32[]{:S(2)}, u32[]{:S(2)}) collective-permute-start(bf16[64,1536]{1,0:T(8,128)(2,1)S(1)} %collective-permute-done.1.refs_2_), channel_id=1, source_target_pairs={{0,1},{1,0},{2,3},{3,2},{4,5},{5,4},{6,7},{7,6},{8,9},{9,8},{10,11... | collective-permute-start | bytes 589832 | tf_op jit(solution)/shard_map/ppermute | solution.py:135
  14.3 2.9 %collective-permute-start.7 = (bf16[64,1536]{1,0:T(8,128)(2,1)S(1)}, bf16[64,1536]{1,0:T(8,128)(2,1)S(1)}, u32[]{:S(2)}, u32[]{:S(2)}) collective-permute-start(bf16[64,1536]{1,0:T(8,128)(2,1)S(1)} %collective-permute-done.2.refs_3_), channel_id=1, source_target_pairs={{0,1},{1,0},{2,3},{3,2},{4,5},{5,4},{6,7},{7,6},{8,9},{9,8},{10,11... | collective-permute-start | bytes 589832 | tf_op jit(solution)/shard_map/ppermute | solution.py:135
  15.6 4.8 %collective-permute-start.3 = (bf16[1,64,768]{2,1,0:T(8,128)(2,1)S(1)}, bf16[1,64,768]{2,1,0:T(8,128)(2,1)S(1)}, u32[]{:S(2)}, u32[]{:S(2)}) collective-permute-start(bf16[1,64,768]{2,1,0:T(8,128)(2,1)S(1)} %get-tuple-element.29), channel_id=1, source_target_pairs={{0,8},{8,0},{16,24},{24,16},{1,9},{9,1},{17,25},{25,17},{2,10},{10... | collective-permute-start | bytes 294920 | tf_op jit(solution)/shard_map/ppermute | solution.py:135
  18.0 7.5 %collective-permute-start.10 = (bf16[1,64,768]{2,1,0:T(8,128)(2,1)S(1)}, bf16[1,64,768]{2,1,0:T(8,128)(2,1)S(1)}, u32[]{:S(2)}, u32[]{:S(2)}) collective-permute-start(bf16[1,64,768]{2,1,0:T(8,128)(2,1)S(1)} %get-tuple-element.33), channel_id=1, source_target_pairs={{0,8},{8,0},{16,24},{24,16},{1,9},{9,1},{17,25},{25,17},{2,10},{10... | collective-permute-start | bytes 294920 | tf_op jit(solution)/shard_map/ppermute | solution.py:135
  20.4 6.3 %collective-permute-start.9 = (bf16[64,768]{1,0:T(8,128)(2,1)S(1)}, bf16[64,768]{1,0:T(8,128)(2,1)S(1)}, u32[]{:S(2)}, u32[]{:S(2)}) collective-permute-start(bf16[64,768]{1,0:T(8,128)(2,1)S(1)} %fusion), channel_id=1, source_target_pairs={{0,16},{8,24},{16,0},{24,8},{1,17},{9,25},{17,1},{25,9},{2,18},{10... | collective-permute-start | bytes 294920 | tf_op jit(solution)/shard_map/ppermute | solution.py:135
  23.1 9.0 %collective-permute-start.8 = (bf16[128,768]{1,0:T(8,128)(2,1)S(1)}, bf16[128,768]{1,0:T(8,128)(2,1)S(1)}, u32[]{:S(2)}, u32[]{:S(2)}) collective-permute-start(bf16[128,768]{1,0:T(8,128)(2,1)S(1)} %pad_maximum_fusion), channel_id=1, source_target_pairs={{0,8},{8,0},{16,24},{24,16},{1,9},{9,1},{17,25},{25,17},{2,10},{10... | collective-permute-start | bytes 589832 | tf_op jit(solution)/shard_map/ppermute | solution.py:135
  25.5 6.6 %collective-permute-start.11 = (bf16[64,768]{1,0:T(8,128)(2,1)S(1)}, bf16[64,768]{1,0:T(8,128)(2,1)S(1)}, u32[]{:S(2)}, u32[]{:S(2)}) collective-permute-start(bf16[64,768]{1,0:T(8,128)(2,1)S(1)} %fusion.1), channel_id=1, source_target_pairs={{0,16},{8,24},{16,0},{24,8},{1,17},{9,25},{17,1},{25,9},{2,18},{10... | collective-permute-start | bytes 294920 | tf_op jit(solution)/shard_map/ppermute | solution.py:135

commit v4 on v2

v4 whole, which is shorter than its diff:
```python
import functools

import jax
import jax.numpy as jnp
from jax import lax
from jax.experimental import pallas as pl
from jax.experimental.pallas import tpu as pltpu
from jax.sharding import PartitionSpec as P

TILE = 96
CON_TILES = 16
RES_TILES = 8
LANES = 128
PERIOD = 384
LINES = TILE * TILE // PERIOD
PIECES = 6
CON = CON_TILES * TILE
RES = RES_TILES * TILE


def densify_kernel(
    map_hbm, tiles_hbm, dense_ref, tiles_ref, flat_ref, square_ref, map_ref, slot_ref, sems
):
    slots = tiles_ref.shape[0]
    width = tiles_ref.shape[1] // PIECES
    map_copy = pltpu.make_async_copy(map_hbm, map_ref, sems.at[PIECES])
    copies = [
        pltpu.make_async_copy(
            tiles_hbm.at[:, pl.ds(i * width, width)],
            tiles_ref.at[:, pl.ds(i * width, width)],
            sems.at[i],
        )
        for i in range(PIECES)
    ]
    map_copy.start()
    for copy in copies:
        copy.start()

    def clear(pair, carry):
        slot_ref[pair] = slots
        return carry

    lax.fori_loop(0, CON_TILES * RES_TILES + 1, clear, 0, unroll=16)
    empty = pl.ds(slots * TILE, TILE)
    square_ref[empty, :] = jnp.zeros((TILE, LANES), jnp.float32)
    map_copy.wait()

    def invert(slot, carry):
        slot_ref[map_ref[slot]] = slot
        return carry

    lax.fori_loop(0, slots, invert, 0, unroll=8)
    for i, copy in enumerate(copies):
        copy.wait()
        for line in range(i * 3 * LINES // PIECES, (i + 1) * 3 * LINES // PIECES):
            flat_ref[line % 3, pl.ds(line // 3, slots, stride=LINES), :] = tiles_ref[
                :, line * LANES : (line + 1) * LANES
            ].astype(jnp.float32)
    x0, x1, x2 = [flat_ref[i, : slots * LINES] for i in range(3)]
    lane = lax.broadcasted_iota(jnp.int32, x0.shape, 1)
    parts = (
        x0,
        pltpu.roll(jnp.where(lane >= 96, x0, x1), 32, 1),
        pltpu.roll(jnp.where(lane >= 64, x1, x2), 64, 1),
        pltpu.roll(x2, 96, 1),
    )
    for i, part in enumerate(parts):
        square_ref[pl.ds(i, slots * LINES, stride=4), :] = part
    lane = lax.broadcasted_iota(jnp.int32, (TILE, LANES), 1)

    def place(con, carry):
        rows = pl.ds(pl.multiple_of(con * TILE, TILE), TILE)
        for half in range(2):
            p = []
            for i in range(4):
                at = slot_ref[con * RES_TILES + 4 * half + i] * TILE
                tile = square_ref[pl.ds(pl.multiple_of(at, TILE), TILE), :]
                p.append(pltpu.roll(tile, LANES - 32 * i, 1) if i else tile)
            out = (
                jnp.where(lane < 96, p[0], p[1]),
                jnp.where(lane < 64, p[1], p[2]),
                jnp.where(lane < 32, p[2], p[3]),
            )
            for i in range(3):
                at = (3 * half + i) * LANES
                dense_ref[rows, at : at + LANES] = out[i].astype(jnp.bfloat16)
        return carry

    lax.fori_loop(0, CON_TILES, place, 0, unroll=True)


def densify(tiles, tile_map):
    slots = tiles.shape[2]
    return pl.pallas_call(
        densify_kernel,
        out_shape=jax.ShapeDtypeStruct((CON, RES), jnp.bfloat16),
        in_specs=[pl.BlockSpec(memory_space=pltpu.HBM)] * 2,
        out_specs=pl.BlockSpec(memory_space=pltpu.VMEM),
        scratch_shapes=[
            pltpu.VMEM((slots, TILE * TILE), jnp.bfloat16),
            pltpu.VMEM((3, (slots + 1) * LINES, LANES), jnp.float32),
            pltpu.VMEM(((slots + 1) * TILE, LANES), jnp.float32),
            pltpu.SMEM((slots,), jnp.int32),
            pltpu.SMEM((CON_TILES * RES_TILES + 8,), jnp.int32),
            pltpu.SemaphoreType.DMA((PIECES + 1,)),
        ],
        compiler_params=pltpu.CompilerParams(vmem_limit_bytes=24 * 2**20),
        cost_estimate=pl.CostEstimate(flops=6 * 10**8, bytes_accessed=0, transcendentals=0),
        name="densify",
    )(
        pltpu.with_memory_space_constraint(tile_map.reshape(slots), pltpu.HBM),
        pltpu.with_memory_space_constraint(tiles.reshape(slots, TILE * TILE), pltpu.HBM),
    )


def ladder_kernel(chips, *refs):
    blocks, dense_ref = refs[:chips], refs[chips]
    outs, rows_ref = refs[chips + 1 : -1], refs[-1]
    chip, occ = lax.axis_index("vir") // 2, lax.axis_index("occ")
    for m in range(chips):
        rows_ref[jnp.bitwise_xor(jnp.bitwise_xor(chip, m), occ)] = blocks[m][...]
    height = rows_ref.shape[1]
    for k in range(0, chips, 4):
        lhs = rows_ref[k : k + 4].reshape(4 * height, CON)
        out = jnp.dot(lhs, dense_ref[...], preferred_element_type=jnp.float32)
        out = out.astype(jnp.bfloat16).reshape(4, height, RES)
        for i in range(4):
            outs[k + i][...] = out[i]


def ladder(blocks, dense):
    chips = len(blocks)
    height = blocks[0].shape[0]
    vmem = pl.BlockSpec(memory_space=pltpu.VMEM)
    return pl.pallas_call(
        functools.partial(ladder_kernel, chips),
        out_shape=[jax.ShapeDtypeStruct((height, RES), jnp.bfloat16)] * chips,
        in_specs=[vmem] * (chips + 1),
        out_specs=[vmem] * chips,
        scratch_shapes=[pltpu.VMEM((chips, height, CON), jnp.bfloat16)],
        compiler_params=pltpu.CompilerParams(vmem_limit_bytes=32 * 2**20),
        cost_estimate=pl.CostEstimate(flops=10**11, bytes_accessed=0, transcendentals=0),
        name="ladder",
    )(*blocks, dense)


def swap(value, axis, size, mask):
    return lax.ppermute(value, axis, [(i, i ^ mask) for i in range(size)])


def add(*terms):
    return sum(term.astype(jnp.float32) for term in terms)


def per_device(n_occ, n_vir, amplitudes, tiles, tile_map):
    chips = n_vir // 2
    height = amplitudes.shape[0]
    swap_occ = functools.partial(swap, axis="occ", size=n_occ)
    swap_vir = functools.partial(swap, axis="vir", size=n_vir)
    dense = densify(tiles, tile_map)
    held = [amplitudes] + [None] * (chips - 1)
    for m in range(chips - 1, 0, -1):
        held[m] = swap_vir(amplitudes, mask=2 * m)
    dense, *held[1:] = lax.optimization_barrier((dense, *held[1:]))
    sibling = swap_vir(amplitudes, mask=1)
    dense, sibling = lax.optimization_barrier((dense, sibling))
    first = ladder(held, dense)
    first, *held[1:] = lax.optimization_barrier((first, *held[1:]))
    rest = swap_vir(jnp.concatenate(held[1:], axis=0), mask=1)
    other = [sibling] + [rest[(m - 1) * height : m * height] for m in range(1, chips)]
    second = ladder(other, dense)
    got = [{k: swap_occ(part[k + 1], mask=1) for k in range(2, n_occ, 2)} for part in (first, second)]
    near = [first[1], second[1]]
    near[1], got[1] = lax.optimization_barrier((near[1], got[1]))
    near = swap_occ(jnp.concatenate(near, axis=0), mask=1)
    near = [near[:height], near[height:]]
    pairs = [
        {k: add(part[k], pair).astype(jnp.bfloat16) for k, pair in received.items()}
        for part, received in zip((first, second), got)
    ]
    sums = [[swap_occ(pair, mask=k) for k, pair in part.items()] for part in pairs]
    first, second = [
        add(part[0], near[i], *sums[i]).astype(jnp.bfloat16) for i, part in enumerate((first, second))
    ]
    core = lax.rem(lax.axis_index("vir"), 2)
    return jnp.where(
        core == 0,
        jnp.concatenate([first, second], axis=0),
        jnp.concatenate([second, first], axis=0),
    )


def solution(mesh):
    in_specs = (P("vir", "occ"), P("occ", "vir", None, None), P("occ", "vir", None))
    out_specs = P("occ", "vir")
    return jax.shard_map(
        functools.partial(per_device, mesh.shape["occ"], mesh.shape["vir"]),
        mesh=mesh,
        in_specs=in_specs,
        out_specs=out_specs,
        check_vma=False,
    )
```

time: 35 us -> 32.9 us (0.940)
  local copies, waits for them, and re-layouts: 1.83 us -> 0.04 us
  starting transfers between devices: 13.3 us -> 14.6 us
  waiting for transfers between devices: 13.9 us -> 12.8 us
  Pallas kernels: 4.78 us -> 4.25 us
    unnamed x6 -> x2, local copies, waits for them, and re-layouts: 1.83 us -> 0.01 us
    ppermute x12 -> x10, starting transfers between devices: 13.3 us -> 14.6 us  [swap(): return lax.ppermute(value, axis, [(i, i ^ mask) for i in range(size)])]
    ppermute x12 -> x10, waiting for transfers between devices: 13.9 us -> 12.8 us  [swap(): return lax.ppermute(value, axis, [(i, i ^ mask) for i in range(size)])]
    pallas_call x1, Pallas kernels: 3.17 us -> 2.63 us  [densify(): pl.pallas_call(densify_kernel, out_shape=jax.ShapeDtypeStruct((CON, RES),...]
  transfers between devices with their start and end apart: 12 -> 10, of which waited for: 5 -> 7; matrix products, arithmetic and copies ran while one was open for 0% -> 0% of each run, Pallas kernels for 11% -> 11%
where the time goes in v4:
time: 32.9 us; the launch traced here: 32.7 us
  starting transfers between devices  14.6 us (44%)
  waiting for transfers between devices  12.8 us (39%)
  Pallas kernels  4.25 us (13%)
  other arithmetic  0.9 us (3%)
    ppermute x10, starting transfers between devices, swap(): return lax.ppermute(value, axis, [(i, i ^ mask) for i in range(size)])  14.6 us
    ppermute x10, waiting for transfers between devices, swap(): return lax.ppermute(value, axis, [(i, i ^ mask) for i in range(size)])  12.8 us
    pallas_call x1, Pallas kernels, densify(): pl.pallas_call(densify_kernel, out_shape=jax.ShapeDtypeStruct((CON, RES),...  2.63 us
    pallas_call x2, Pallas kernels, ladder(): pl.pallas_call(functools.partial(ladder_kernel, chips), out_shape=[jax.Sh...  1.62 us
    select_n x1, other arithmetic, per_device(): jnp.where(core == 0, jnp.concatenate([first, second], axis=0), jnp.concat...  0.72 us
  transfers between devices with their start and end apart: 10, of which 7 were waited for; matrix products, arithmetic and copies ran while one was open for 0% of the time, Pallas kernels for 11%

profile of v4, /device:TPU:0, one launch (start us, length us, event | category | flops | bytes accessed | tf_op | source)
XLA Modules:
  0.0 32.7 jit_solution(4961098699591103138)
XLA Ops:
  0.0 2.9 %collective-permute-start = (bf16[64,1536]{1,0:T(8,128)(2,1)}, bf16[64,1536]{1,0:T(8,128)(2,1)S(1)}, u32[]{:S(2)}, u32[]{:S(2)}) collective-permute-start(bf16[64,1536]{1,0:T(8,128)(2,1)} %refs_0_.1), channel_id=1, source_target_pairs={{0,2},{1,3},{2,0},{3,1},{4,6},{5,7},{6,4},{7,5},{8,10},{9,11},{10,... | collective-permute-start | bytes 589832 | tf_op jit(solution)/shard_map/ppermute | solution.py:148
  2.9 1.5 %collective-permute-start.1 = (bf16[64,1536]{1,0:T(8,128)(2,1)}, bf16[64,1536]{1,0:T(8,128)(2,1)S(1)}, u32[]{:S(2)}, u32[]{:S(2)}) collective-permute-start(bf16[64,1536]{1,0:T(8,128)(2,1)} %refs_0_.1), channel_id=1, source_target_pairs={{0,4},{1,5},{2,6},{3,7},{4,0},{5,1},{6,2},{7,3},{8,12},{9,13},{10,... | collective-permute-start | bytes 589832 | tf_op jit(solution)/shard_map/ppermute | solution.py:148
  4.5 0.0 collective-permute-start.2
  4.5 0.0 collective-permute-start.3
  4.5 2.6 %densify.1.refs_4_ = bf16[1536,768]{1,0:T(8,128)(2,1)S(1)} custom-call(s32[48]{0:T(128)} %bitcast.3, bf16[48,9216]{1,0:T(8,128)(2,1)} %bitcast.2), custom_call_target="tpu_custom_call" | custom-call | flops 600000000 | tf_op jit(solution)/shard_map/densify/pallas_call | solution.py:94
  7.1 1.8 %collective-permute-done.refs_1_ = bf16[64,1536]{1,0:T(8,128)(2,1)S(1)} collective-permute-done((bf16[64,1536]{1,0:T(8,128)(2,1)}, bf16[64,1536]{1,0:T(8,128)(2,1)S(1)}, u32[]{:S(2)}, u32[]{:S(2)}) %collective-permute-start) | collective-permute-done | bytes 196640 | tf_op jit(solution)/shard_map/ppermute | solution.py:148
  8.9 4.8 %collective-permute-done.1.refs_2_ = bf16[64,1536]{1,0:T(8,128)(2,1)S(1)} collective-permute-done((bf16[64,1536]{1,0:T(8,128)(2,1)}, bf16[64,1536]{1,0:T(8,128)(2,1)S(1)}, u32[]{:S(2)}, u32[]{:S(2)}) %collective-permute-start.1) | collective-permute-done | bytes 196640 | tf_op jit(solution)/shard_map/ppermute | solution.py:148
  13.7 0.0 collective-permute-done.2.refs_3_
  13.7 0.0 collective-permute-done.3.refs_0_
  13.7 0.8 %ladder.2 = (bf16[64,768]{1,0:T(8,128)(2,1)S(1)}, bf16[64,768]{1,0:T(8,128)(2,1)S(1)}, bf16[64,768]{1,0:T(8,128)(2,1)S(1)}, bf16[64,768]{1,0:T(8,128)(2,1)S(1)}) custom-call(bf16[64,1536]{1,0:T(8,128)(2,1)S(1)} %copy-done, bf16[64,1536]{1,0:T(8,128)(2,1)S(1)} %collective-permute-done.refs_1_, bf16[64,1536]{1,0:T(8,128)(2,1)S(1)} %collective-permute-done.1.refs_2_, ...), custom_call_target="tpu_custom_call" | custom-call | flops 99999997952 | tf_op jit(solution)/shard_map/ladder/pallas_call | solution.py:135
  14.6 0.1 collective-permute-start.4
  14.7 1.6 %collective-permute-start.7 = (bf16[64,768]{1,0:T(8,128)(2,1)S(1)}, bf16[64,768]{1,0:T(8,128)(2,1)S(1)}, u32[]{:S(2)}, u32[]{:S(2)}) collective-permute-start(bf16[64,768]{1,0:T(8,128)(2,1)S(1)} %get-tuple-element.47), channel_id=1, source_target_pairs={{0,8},{8,0},{16,24},{24,16},{1,9},{9,1},{17,25},{25,17},{2,10},{10... | collective-permute-start | bytes 294920 | tf_op jit(solution)/shard_map/ppermute | solution.py:148
  16.3 0.3 %collective-permute-done.4 = bf16[192,1536]{1,0:T(8,128)(2,1)S(1)} collective-permute-done((bf16[192,1536]{1,0:T(8,128)(2,1)S(1)}, bf16[192,1536]{1,0:T(8,128)(2,1)S(1)}, u32[]{:S(2)}, u32[]{:S(2)}) %collective-permute-start.4) | collective-permute-done | bytes 589856 | tf_op jit(solution)/shard_map/ppermute | solution.py:148
  16.7 0.8 %ladder.3 = (bf16[64,768]{1,0:T(8,128)(2,1)S(1)}, bf16[64,768]{1,0:T(8,128)(2,1)S(1)}, bf16[64,768]{1,0:T(8,128)(2,1)S(1)}, bf16[64,768]{1,0:T(8,128)(2,1)S(1)}) custom-call(bf16[64,1536]{1,0:T(8,128)(2,1)S(1)} %collective-permute-done.3.refs_0_, bf16[64,1536]{1,0:T(8,128)(2,1)S(1)} %get-tuple-element.53.refs_1_, ...), custom_call_target="tpu_custom_call" | custom-call | flops 99999997952 | tf_op jit(solution)/shard_map/ladder/pallas_call | solution.py:135
  17.5 1.6 %collective-permute-start.5 = (bf16[64,768]{1,0:T(8,128)(2,1)S(1)}, bf16[64,768]{1,0:T(8,128)(2,1)S(1)}, u32[]{:S(2)}, u32[]{:S(2)}) collective-permute-start(bf16[64,768]{1,0:T(8,128)(2,1)S(1)} %get-tuple-element.44), channel_id=1, source_target_pairs={{0,8},{8,0},{16,24},{24,16},{1,9},{9,1},{17,25},{25,17},{2,10},{10... | collective-permute-start | bytes 294920 | tf_op jit(solution)/shard_map/ppermute | solution.py:148
  19.2 0.7 %collective-permute-done.7 = bf16[64,768]{1,0:T(8,128)(2,1)S(1)} collective-permute-done((bf16[64,768]{1,0:T(8,128)(2,1)S(1)}, bf16[64,768]{1,0:T(8,128)(2,1)S(1)}, u32[]{:S(2)}, u32[]{:S(2)}) %collective-permute-start.7) | collective-permute-done | bytes 98336 | tf_op jit(solution)/shard_map/ppermute | solution.py:148
  19.9 2.7 %collective-permute-start.8 = (bf16[64,768]{1,0:T(8,128)(2,1)S(1)}, bf16[64,768]{1,0:T(8,128)(2,1)S(1)}, u32[]{:S(2)}, u32[]{:S(2)}) collective-permute-start(bf16[64,768]{1,0:T(8,128)(2,1)S(1)} %add_convert_fusion.3), channel_id=1, source_target_pairs={{0,16},{8,24},{16,0},{24,8},{1,17},{9,25},{17,1},{25,9},{2,18},{10... | collective-permute-start | bytes 294920 | tf_op jit(solution)/shard_map/ppermute | solution.py:148
  22.6 1.6 %collective-permute-start.6 = (bf16[128,768]{1,0:T(8,128)(2,1)S(1)}, bf16[128,768]{1,0:T(8,128)(2,1)S(1)}, u32[]{:S(2)}, u32[]{:S(2)}) collective-permute-start(bf16[128,768]{1,0:T(8,128)(2,1)S(1)} %pad_maximum_fusion.1), channel_id=1, source_target_pairs={{0,8},{8,0},{16,24},{24,16},{1,9},{9,1},{17,25},{25,17},{2,10},{10... | collective-permute-start | bytes 589832 | tf_op jit(solution)/shard_map/ppermute | solution.py:148
  24.3 2.5 %collective-permute-start.9 = (bf16[64,768]{1,0:T(8,128)(2,1)S(1)}, bf16[64,768]{1,0:T(8,128)(2,1)S(1)}, u32[]{:S(2)}, u32[]{:S(2)}) collective-permute-start(bf16[64,768]{1,0:T(8,128)(2,1)S(1)} %add_convert_fusion.1), channel_id=1, source_target_pairs={{0,16},{8,24},{16,0},{24,8},{1,17},{9,25},{17,1},{25,9},{2,18},{10... | collective-permute-start | bytes 294920 | tf_op jit(solution)/shard_map/ppermute | solution.py:148
  26.8 1.2 %collective-permute-done.8 = bf16[64,768]{1,0:T(8,128)(2,1)S(1)} collective-permute-done((bf16[64,768]{1,0:T(8,128)(2,1)S(1)}, bf16[64,768]{1,0:T(8,128)(2,1)S(1)}, u32[]{:S(2)}, u32[]{:S(2)}) %collective-permute-start.8) | collective-permute-done | bytes 98336 | tf_op jit(solution)/shard_map/ppermute | solution.py:148
  28.0 3.1 %collective-permute-done.9 = bf16[64,768]{1,0:T(8,128)(2,1)S(1)} collective-permute-done((bf16[64,768]{1,0:T(8,128)(2,1)S(1)}, bf16[64,768]{1,0:T(8,128)(2,1)S(1)}, u32[]{:S(2)}, u32[]{:S(2)}) %collective-permute-start.9) | collective-permute-done | bytes 98336 | tf_op jit(solution)/shard_map/ppermute | solution.py:148
  31.0 0.9 %collective-permute-done.6 = bf16[128,768]{1,0:T(8,128)(2,1)S(1)} collective-permute-done((bf16[128,768]{1,0:T(8,128)(2,1)S(1)}, bf16[128,768]{1,0:T(8,128)(2,1)S(1)}, u32[]{:S(2)}, u32[]{:S(2)}) %collective-permute-start.6) | collective-permute-done | bytes 196640 | tf_op jit(solution)/shard_map/ppermute | solution.py:148
  31.9 0.1 add_convert_fusion.2
  32.0 0.7 %maximum_select_fusion = bf16[128,768]{1,0:T(8,128)(2,1)} fusion(bf16[64,768]{1,0:T(8,128)(2,1)S(1)} %get-tuple-element.55, bf16[64,768]{1,0:T(8,128)(2,1)S(1)} %get-tuple-element.54, pred[]{:T(512)S(6)} %eq.3), kind=kLoop, calls=%fused_computation.2 | loop fusion | flops 884736 | bytes 393217 | tf_op jit(solution)/shard_map/jit(_where)/select_n | solution.py:186
  (8 shorter events, 0.2 us)
Async XLA Ops:
  0.0 8.9 %collective-permute-start = (bf16[64,1536]{1,0:T(8,128)(2,1)}, bf16[64,1536]{1,0:T(8,128)(2,1)S(1)}, u32[]{:S(2)}, u32[]{:S(2)}) collective-permute-start(bf16[64,1536]{1,0:T(8,128)(2,1)} %refs_0_.1), channel_id=1, source_target_pairs={{0,2},{1,3},{2,0},{3,1},{4,6},{5,7},{6,4},{7,5},{8,10},{9,11},{10,... | collective-permute-start | bytes 589832 | tf_op jit(solution)/shard_map/ppermute | solution.py:148
  2.9 10.8 %collective-permute-start.1 = (bf16[64,1536]{1,0:T(8,128)(2,1)}, bf16[64,1536]{1,0:T(8,128)(2,1)S(1)}, u32[]{:S(2)}, u32[]{:S(2)}) collective-permute-start(bf16[64,1536]{1,0:T(8,128)(2,1)} %refs_0_.1), channel_id=1, source_target_pairs={{0,4},{1,5},{2,6},{3,7},{4,0},{5,1},{6,2},{7,3},{8,12},{9,13},{10,... | collective-permute-start | bytes 589832 | tf_op jit(solution)/shard_map/ppermute | solution.py:148
  4.5 9.3 %collective-permute-start.2 = (bf16[64,1536]{1,0:T(8,128)(2,1)}, bf16[64,1536]{1,0:T(8,128)(2,1)S(1)}, u32[]{:S(2)}, u32[]{:S(2)}) collective-permute-start(bf16[64,1536]{1,0:T(8,128)(2,1)} %refs_0_.1), channel_id=1, source_target_pairs={{0,6},{1,7},{2,4},{3,5},{4,2},{5,3},{6,0},{7,1},{8,14},{9,15},{10,... | collective-permute-start | bytes 589832 | tf_op jit(solution)/shard_map/ppermute | solution.py:148
  4.5 9.3 %collective-permute-start.3 = (bf16[64,1536]{1,0:T(8,128)(2,1)}, bf16[64,1536]{1,0:T(8,128)(2,1)S(1)}, u32[]{:S(2)}, u32[]{:S(2)}) collective-permute-start(bf16[64,1536]{1,0:T(8,128)(2,1)} %refs_0_.1), channel_id=1, source_target_pairs={{0,1},{1,0},{2,3},{3,2},{4,5},{5,4},{6,7},{7,6},{8,9},{9,8},{10,11... | collective-permute-start | bytes 589832 | tf_op jit(solution)/shard_map/ppermute | solution.py:148
  4.5 9.3 %copy-start = (bf16[64,1536]{1,0:T(8,128)(2,1)S(1)}, bf16[64,1536]{1,0:T(8,128)(2,1)}, u32[]{:S(2)}) copy-start(bf16[64,1536]{1,0:T(8,128)(2,1)} %refs_0_.1) | copy-start | bytes 589828
  14.6 2.1 %collective-permute-start.4 = (bf16[192,1536]{1,0:T(8,128)(2,1)S(1)}, bf16[192,1536]{1,0:T(8,128)(2,1)S(1)}, u32[]{:S(2)}, u32[]{:S(2)}) collective-permute-start(bf16[192,1536]{1,0:T(8,128)(2,1)S(1)} %pad_maximum_fusion), channel_id=1, source_target_pairs={{0,1},{1,0},{2,3},{3,2},{4,5},{5,4},{6,7},{7,6},{8,9},{9,8},{10,11... | collective-permute-start | bytes 1769480 | tf_op jit(solution)/shard_map/ppermute | solution.py:148
  14.7 5.2 %collective-permute-start.7 = (bf16[64,768]{1,0:T(8,128)(2,1)S(1)}, bf16[64,768]{1,0:T(8,128)(2,1)S(1)}, u32[]{:S(2)}, u32[]{:S(2)}) collective-permute-start(bf16[64,768]{1,0:T(8,128)(2,1)S(1)} %get-tuple-element.47), channel_id=1, source_target_pairs={{0,8},{8,0},{16,24},{24,16},{1,9},{9,1},{17,25},{25,17},{2,10},{10... | collective-permute-start | bytes 294920 | tf_op jit(solution)/shard_map/ppermute | solution.py:148
  17.5 5.0 %collective-permute-start.5 = (bf16[64,768]{1,0:T(8,128)(2,1)S(1)}, bf16[64,768]{1,0:T(8,128)(2,1)S(1)}, u32[]{:S(2)}, u32[]{:S(2)}) collective-permute-start(bf16[64,768]{1,0:T(8,128)(2,1)S(1)} %get-tuple-element.44), channel_id=1, source_target_pairs={{0,8},{8,0},{16,24},{24,16},{1,9},{9,1},{17,25},{25,17},{2,10},{10... | collective-permute-start | bytes 294920 | tf_op jit(solution)/shard_map/ppermute | solution.py:148
  19.9 8.0 %collective-permute-start.8 = (bf16[64,768]{1,0:T(8,128)(2,1)S(1)}, bf16[64,768]{1,0:T(8,128)(2,1)S(1)}, u32[]{:S(2)}, u32[]{:S(2)}) collective-permute-start(bf16[64,768]{1,0:T(8,128)(2,1)S(1)} %add_convert_fusion.3), channel_id=1, source_target_pairs={{0,16},{8,24},{16,0},{24,8},{1,17},{9,25},{17,1},{25,9},{2,18},{10... | collective-permute-start | bytes 294920 | tf_op jit(solution)/shard_map/ppermute | solution.py:148
  22.6 9.3 %collective-permute-start.6 = (bf16[128,768]{1,0:T(8,128)(2,1)S(1)}, bf16[128,768]{1,0:T(8,128)(2,1)S(1)}, u32[]{:S(2)}, u32[]{:S(2)}) collective-permute-start(bf16[128,768]{1,0:T(8,128)(2,1)S(1)} %pad_maximum_fusion.1), channel_id=1, source_target_pairs={{0,8},{8,0},{16,24},{24,16},{1,9},{9,1},{17,25},{25,17},{2,10},{10... | collective-permute-start | bytes 589832 | tf_op jit(solution)/shard_map/ppermute | solution.py:148
  24.3 6.8 %collective-permute-start.9 = (bf16[64,768]{1,0:T(8,128)(2,1)S(1)}, bf16[64,768]{1,0:T(8,128)(2,1)S(1)}, u32[]{:S(2)}, u32[]{:S(2)}) collective-permute-start(bf16[64,768]{1,0:T(8,128)(2,1)S(1)} %add_convert_fusion.1), channel_id=1, source_target_pairs={{0,16},{8,24},{16,0},{24,8},{1,17},{9,25},{17,1},{25,9},{2,18},{10... | collective-permute-start | bytes 294920 | tf_op jit(solution)/shard_map/ppermute | solution.py:148

commit v5 on v4

--- a/solution.py
+++ b/solution.py
@@ -183,11 +183,8 @@
         add(part[0], near[i], *sums[i]).astype(jnp.bfloat16) for i, part in enumerate((first, second))
     ]
     core = lax.rem(lax.axis_index("vir"), 2)
-    return jnp.where(
-        core == 0,
-        jnp.concatenate([first, second], axis=0),
-        jnp.concatenate([second, first], axis=0),
-    )
+    top, bottom = jnp.where(core == 0, first, second), jnp.where(core == 0, second, first)
+    return jnp.concatenate([top, bottom], axis=0)
 
 
 def solution(mesh):

time: 32.9 us -> 32.8 us (level)
  other arithmetic: 0.9 us -> 0.19 us
  local copies, waits for them, and re-layouts: 0.04 us -> 0.71 us
    unnamed x2 -> x4, local copies, waits for them, and re-layouts: 0.01 us -> 0.68 us
    select_n x1 -> x2, other arithmetic: 0.72 us -> 0.09 us  [per_device(): jnp.where(core == 0, first, second)]
where the time goes in v5:
time: 32.8 us; the launch traced here: 32.7 us
  starting transfers between devices  14.6 us (45%)
  waiting for transfers between devices  12.8 us (39%)
  Pallas kernels  4.25 us (13%)
  local copies, waits for them, and re-layouts  0.71 us (2%)
    ppermute x10, starting transfers between devices, swap(): return lax.ppermute(value, axis, [(i, i ^ mask) for i in range(size)])  14.6 us
    ppermute x10, waiting for transfers between devices, swap(): return lax.ppermute(value, axis, [(i, i ^ mask) for i in range(size)])  12.8 us
    pallas_call x1, Pallas kernels, densify(): pl.pallas_call(densify_kernel, out_shape=jax.ShapeDtypeStruct((CON, RES),...  2.63 us
    pallas_call x2, Pallas kernels, ladder(): pl.pallas_call(functools.partial(ladder_kernel, chips), out_shape=[jax.Sh...  1.62 us
    unnamed x4, local copies, waits for them, and re-layouts  0.68 us
  transfers between devices with their start and end apart: 10, of which 7 were waited for; matrix products, arithmetic and copies ran while one was open for 0% of the time, Pallas kernels for 11%

profile of v5, /device:TPU:0, one launch (start us, length us, event | category | flops | bytes accessed | tf_op | source)
XLA Modules:
  0.0 32.7 jit_solution(5506436064154874698)
XLA Ops:
  0.0 2.9 %collective-permute-start = (bf16[64,1536]{1,0:T(8,128)(2,1)}, bf16[64,1536]{1,0:T(8,128)(2,1)S(1)}, u32[]{:S(2)}, u32[]{:S(2)}) collective-permute-start(bf16[64,1536]{1,0:T(8,128)(2,1)} %refs_0_.1), channel_id=1, source_target_pairs={{0,2},{1,3},{2,0},{3,1},{4,6},{5,7},{6,4},{7,5},{8,10},{9,11},{10,... | collective-permute-start | bytes 589832 | tf_op jit(solution)/shard_map/ppermute | solution.py:148
  2.9 1.5 %collective-permute-start.1 = (bf16[64,1536]{1,0:T(8,128)(2,1)}, bf16[64,1536]{1,0:T(8,128)(2,1)S(1)}, u32[]{:S(2)}, u32[]{:S(2)}) collective-permute-start(bf16[64,1536]{1,0:T(8,128)(2,1)} %refs_0_.1), channel_id=1, source_target_pairs={{0,4},{1,5},{2,6},{3,7},{4,0},{5,1},{6,2},{7,3},{8,12},{9,13},{10,... | collective-permute-start | bytes 589832 | tf_op jit(solution)/shard_map/ppermute | solution.py:148
  4.5 0.0 collective-permute-start.2
  4.5 0.0 collective-permute-start.3
  4.5 2.6 %densify.1.refs_4_ = bf16[1536,768]{1,0:T(8,128)(2,1)S(1)} custom-call(s32[48]{0:T(128)} %bitcast.3, bf16[48,9216]{1,0:T(8,128)(2,1)} %bitcast.2), custom_call_target="tpu_custom_call" | custom-call | flops 600000000 | tf_op jit(solution)/shard_map/densify/pallas_call | solution.py:94
  7.1 1.8 %collective-permute-done.refs_1_ = bf16[64,1536]{1,0:T(8,128)(2,1)S(1)} collective-permute-done((bf16[64,1536]{1,0:T(8,128)(2,1)}, bf16[64,1536]{1,0:T(8,128)(2,1)S(1)}, u32[]{:S(2)}, u32[]{:S(2)}) %collective-permute-start) | collective-permute-done | bytes 196640 | tf_op jit(solution)/shard_map/ppermute | solution.py:148
  8.9 4.8 %collective-permute-done.1.refs_2_ = bf16[64,1536]{1,0:T(8,128)(2,1)S(1)} collective-permute-done((bf16[64,1536]{1,0:T(8,128)(2,1)}, bf16[64,1536]{1,0:T(8,128)(2,1)S(1)}, u32[]{:S(2)}, u32[]{:S(2)}) %collective-permute-start.1) | collective-permute-done | bytes 196640 | tf_op jit(solution)/shard_map/ppermute | solution.py:148
  13.7 0.0 collective-permute-done.3.refs_0_
  13.7 0.8 %ladder.2 = (bf16[64,768]{1,0:T(8,128)(2,1)S(1)}, bf16[64,768]{1,0:T(8,128)(2,1)S(1)}, bf16[64,768]{1,0:T(8,128)(2,1)S(1)}, bf16[64,768]{1,0:T(8,128)(2,1)S(1)}) custom-call(bf16[64,1536]{1,0:T(8,128)(2,1)S(1)} %copy-done, bf16[64,1536]{1,0:T(8,128)(2,1)S(1)} %collective-permute-done.refs_1_, bf16[64,1536]{1,0:T(8,128)(2,1)S(1)} %collective-permute-done.1.refs_2_, ...), custom_call_target="tpu_custom_call" | custom-call | flops 99999997952 | tf_op jit(solution)/shard_map/ladder/pallas_call | solution.py:135
  14.6 0.1 collective-permute-start.4
  14.7 1.6 %collective-permute-start.7 = (bf16[64,768]{1,0:T(8,128)(2,1)S(1)}, bf16[64,768]{1,0:T(8,128)(2,1)S(1)}, u32[]{:S(2)}, u32[]{:S(2)}) collective-permute-start(bf16[64,768]{1,0:T(8,128)(2,1)S(1)} %get-tuple-element.47), channel_id=1, source_target_pairs={{0,8},{8,0},{16,24},{24,16},{1,9},{9,1},{17,25},{25,17},{2,10},{10... | collective-permute-start | bytes 294920 | tf_op jit(solution)/shard_map/ppermute | solution.py:148
  16.3 0.3 %collective-permute-done.4 = bf16[192,1536]{1,0:T(8,128)(2,1)S(1)} collective-permute-done((bf16[192,1536]{1,0:T(8,128)(2,1)S(1)}, bf16[192,1536]{1,0:T(8,128)(2,1)S(1)}, u32[]{:S(2)}, u32[]{:S(2)}) %collective-permute-start.4) | collective-permute-done | bytes 589856 | tf_op jit(solution)/shard_map/ppermute | solution.py:148
  16.7 0.8 %ladder.3 = (bf16[64,768]{1,0:T(8,128)(2,1)S(1)}, bf16[64,768]{1,0:T(8,128)(2,1)S(1)}, bf16[64,768]{1,0:T(8,128)(2,1)S(1)}, bf16[64,768]{1,0:T(8,128)(2,1)S(1)}) custom-call(bf16[64,1536]{1,0:T(8,128)(2,1)S(1)} %collective-permute-done.3.refs_0_, bf16[64,1536]{1,0:T(8,128)(2,1)S(1)} %get-tuple-element.55.refs_1_, ...), custom_call_target="tpu_custom_call" | custom-call | flops 99999997952 | tf_op jit(solution)/shard_map/ladder/pallas_call | solution.py:135
  17.5 1.6 %collective-permute-start.5 = (bf16[64,768]{1,0:T(8,128)(2,1)S(1)}, bf16[64,768]{1,0:T(8,128)(2,1)S(1)}, u32[]{:S(2)}, u32[]{:S(2)}) collective-permute-start(bf16[64,768]{1,0:T(8,128)(2,1)S(1)} %get-tuple-element.44), channel_id=1, source_target_pairs={{0,8},{8,0},{16,24},{24,16},{1,9},{9,1},{17,25},{25,17},{2,10},{10... | collective-permute-start | bytes 294920 | tf_op jit(solution)/shard_map/ppermute | solution.py:148
  19.2 0.7 %collective-permute-done.7 = bf16[64,768]{1,0:T(8,128)(2,1)S(1)} collective-permute-done((bf16[64,768]{1,0:T(8,128)(2,1)S(1)}, bf16[64,768]{1,0:T(8,128)(2,1)S(1)}, u32[]{:S(2)}, u32[]{:S(2)}) %collective-permute-start.7) | collective-permute-done | bytes 98336 | tf_op jit(solution)/shard_map/ppermute | solution.py:148
  19.9 2.7 %collective-permute-start.8 = (bf16[64,768]{1,0:T(8,128)(2,1)S(1)}, bf16[64,768]{1,0:T(8,128)(2,1)S(1)}, u32[]{:S(2)}, u32[]{:S(2)}) collective-permute-start(bf16[64,768]{1,0:T(8,128)(2,1)S(1)} %add_convert_fusion.3), channel_id=1, source_target_pairs={{0,16},{8,24},{16,0},{24,8},{1,17},{9,25},{17,1},{25,9},{2,18},{10... | collective-permute-start | bytes 294920 | tf_op jit(solution)/shard_map/ppermute | solution.py:148
  22.6 1.6 %collective-permute-start.6 = (bf16[128,768]{1,0:T(8,128)(2,1)S(1)}, bf16[128,768]{1,0:T(8,128)(2,1)S(1)}, u32[]{:S(2)}, u32[]{:S(2)}) collective-permute-start(bf16[128,768]{1,0:T(8,128)(2,1)S(1)} %pad_maximum_fusion.1), channel_id=1, source_target_pairs={{0,8},{8,0},{16,24},{24,16},{1,9},{9,1},{17,25},{25,17},{2,10},{10... | collective-permute-start | bytes 589832 | tf_op jit(solution)/shard_map/ppermute | solution.py:148
  24.3 2.5 %collective-permute-start.9 = (bf16[64,768]{1,0:T(8,128)(2,1)S(1)}, bf16[64,768]{1,0:T(8,128)(2,1)S(1)}, u32[]{:S(2)}, u32[]{:S(2)}) collective-permute-start(bf16[64,768]{1,0:T(8,128)(2,1)S(1)} %add_convert_fusion.1), channel_id=1, source_target_pairs={{0,16},{8,24},{16,0},{24,8},{1,17},{9,25},{17,1},{25,9},{2,18},{10... | collective-permute-start | bytes 294920 | tf_op jit(solution)/shard_map/ppermute | solution.py:148
  26.8 1.2 %collective-permute-done.8 = bf16[64,768]{1,0:T(8,128)(2,1)S(1)} collective-permute-done((bf16[64,768]{1,0:T(8,128)(2,1)S(1)}, bf16[64,768]{1,0:T(8,128)(2,1)S(1)}, u32[]{:S(2)}, u32[]{:S(2)}) %collective-permute-start.8) | collective-permute-done | bytes 98336 | tf_op jit(solution)/shard_map/ppermute | solution.py:148
  28.0 3.1 %collective-permute-done.9 = bf16[64,768]{1,0:T(8,128)(2,1)S(1)} collective-permute-done((bf16[64,768]{1,0:T(8,128)(2,1)S(1)}, bf16[64,768]{1,0:T(8,128)(2,1)S(1)}, u32[]{:S(2)}, u32[]{:S(2)}) %collective-permute-start.9) | collective-permute-done | bytes 98336 | tf_op jit(solution)/shard_map/ppermute | solution.py:148
  31.0 0.9 %collective-permute-done.6 = bf16[128,768]{1,0:T(8,128)(2,1)S(1)} collective-permute-done((bf16[128,768]{1,0:T(8,128)(2,1)S(1)}, bf16[128,768]{1,0:T(8,128)(2,1)S(1)}, u32[]{:S(2)}, u32[]{:S(2)}) %collective-permute-start.6) | collective-permute-done | bytes 196640 | tf_op jit(solution)/shard_map/ppermute | solution.py:148
  31.9 0.1 broadcast_select_fusion.1
  32.0 0.0 copy-start.1
  32.0 0.7 %copy-done.1 = bf16[128,768]{1,0:T(8,128)(2,1)} copy-done((bf16[128,768]{1,0:T(8,128)(2,1)}, bf16[128,768]{1,0:T(8,128)(2,1)S(1)}, u32[]{:S(2)}) %copy-start.1) | copy-done | bytes 196632
  (10 shorter events, 0.2 us)
Async XLA Ops:
  0.0 8.9 %collective-permute-start = (bf16[64,1536]{1,0:T(8,128)(2,1)}, bf16[64,1536]{1,0:T(8,128)(2,1)S(1)}, u32[]{:S(2)}, u32[]{:S(2)}) collective-permute-start(bf16[64,1536]{1,0:T(8,128)(2,1)} %refs_0_.1), channel_id=1, source_target_pairs={{0,2},{1,3},{2,0},{3,1},{4,6},{5,7},{6,4},{7,5},{8,10},{9,11},{10,... | collective-permute-start | bytes 589832 | tf_op jit(solution)/shard_map/ppermute | solution.py:148
  2.9 10.8 %collective-permute-start.1 = (bf16[64,1536]{1,0:T(8,128)(2,1)}, bf16[64,1536]{1,0:T(8,128)(2,1)S(1)}, u32[]{:S(2)}, u32[]{:S(2)}) collective-permute-start(bf16[64,1536]{1,0:T(8,128)(2,1)} %refs_0_.1), channel_id=1, source_target_pairs={{0,4},{1,5},{2,6},{3,7},{4,0},{5,1},{6,2},{7,3},{8,12},{9,13},{10,... | collective-permute-start | bytes 589832 | tf_op jit(solution)/shard_map/ppermute | solution.py:148
  4.5 9.3 %collective-permute-start.2 = (bf16[64,1536]{1,0:T(8,128)(2,1)}, bf16[64,1536]{1,0:T(8,128)(2,1)S(1)}, u32[]{:S(2)}, u32[]{:S(2)}) collective-permute-start(bf16[64,1536]{1,0:T(8,128)(2,1)} %refs_0_.1), channel_id=1, source_target_pairs={{0,6},{1,7},{2,4},{3,5},{4,2},{5,3},{6,0},{7,1},{8,14},{9,15},{10,... | collective-permute-start | bytes 589832 | tf_op jit(solution)/shard_map/ppermute | solution.py:148
  4.5 9.3 %collective-permute-start.3 = (bf16[64,1536]{1,0:T(8,128)(2,1)}, bf16[64,1536]{1,0:T(8,128)(2,1)S(1)}, u32[]{:S(2)}, u32[]{:S(2)}) collective-permute-start(bf16[64,1536]{1,0:T(8,128)(2,1)} %refs_0_.1), channel_id=1, source_target_pairs={{0,1},{1,0},{2,3},{3,2},{4,5},{5,4},{6,7},{7,6},{8,9},{9,8},{10,11... | collective-permute-start | bytes 589832 | tf_op jit(solution)/shard_map/ppermute | solution.py:148
  4.5 9.3 %copy-start = (bf16[64,1536]{1,0:T(8,128)(2,1)S(1)}, bf16[64,1536]{1,0:T(8,128)(2,1)}, u32[]{:S(2)}) copy-start(bf16[64,1536]{1,0:T(8,128)(2,1)} %refs_0_.1) | copy-start | bytes 589828
  14.6 2.1 %collective-permute-start.4 = (bf16[192,1536]{1,0:T(8,128)(2,1)S(1)}, bf16[192,1536]{1,0:T(8,128)(2,1)S(1)}, u32[]{:S(2)}, u32[]{:S(2)}) collective-permute-start(bf16[192,1536]{1,0:T(8,128)(2,1)S(1)} %pad_maximum_fusion), channel_id=1, source_target_pairs={{0,1},{1,0},{2,3},{3,2},{4,5},{5,4},{6,7},{7,6},{8,9},{9,8},{10,11... | collective-permute-start | bytes 1769480 | tf_op jit(solution)/shard_map/ppermute | solution.py:148
  14.7 5.2 %collective-permute-start.7 = (bf16[64,768]{1,0:T(8,128)(2,1)S(1)}, bf16[64,768]{1,0:T(8,128)(2,1)S(1)}, u32[]{:S(2)}, u32[]{:S(2)}) collective-permute-start(bf16[64,768]{1,0:T(8,128)(2,1)S(1)} %get-tuple-element.47), channel_id=1, source_target_pairs={{0,8},{8,0},{16,24},{24,16},{1,9},{9,1},{17,25},{25,17},{2,10},{10... | collective-permute-start | bytes 294920 | tf_op jit(solution)/shard_map/ppermute | solution.py:148
  17.5 5.0 %collective-permute-start.5 = (bf16[64,768]{1,0:T(8,128)(2,1)S(1)}, bf16[64,768]{1,0:T(8,128)(2,1)S(1)}, u32[]{:S(2)}, u32[]{:S(2)}) collective-permute-start(bf16[64,768]{1,0:T(8,128)(2,1)S(1)} %get-tuple-element.44), channel_id=1, source_target_pairs={{0,8},{8,0},{16,24},{24,16},{1,9},{9,1},{17,25},{25,17},{2,10},{10... | collective-permute-start | bytes 294920 | tf_op jit(solution)/shard_map/ppermute | solution.py:148
  19.9 8.0 %collective-permute-start.8 = (bf16[64,768]{1,0:T(8,128)(2,1)S(1)}, bf16[64,768]{1,0:T(8,128)(2,1)S(1)}, u32[]{:S(2)}, u32[]{:S(2)}) collective-permute-start(bf16[64,768]{1,0:T(8,128)(2,1)S(1)} %add_convert_fusion.3), channel_id=1, source_target_pairs={{0,16},{8,24},{16,0},{24,8},{1,17},{9,25},{17,1},{25,9},{2,18},{10... | collective-permute-start | bytes 294920 | tf_op jit(solution)/shard_map/ppermute | solution.py:148
  22.6 9.3 %collective-permute-start.6 = (bf16[128,768]{1,0:T(8,128)(2,1)S(1)}, bf16[128,768]{1,0:T(8,128)(2,1)S(1)}, u32[]{:S(2)}, u32[]{:S(2)}) collective-permute-start(bf16[128,768]{1,0:T(8,128)(2,1)S(1)} %pad_maximum_fusion.1), channel_id=1, source_target_pairs={{0,8},{8,0},{16,24},{24,16},{1,9},{9,1},{17,25},{25,17},{2,10},{10... | collective-permute-start | bytes 589832 | tf_op jit(solution)/shard_map/ppermute | solution.py:148
  24.3 6.8 %collective-permute-start.9 = (bf16[64,768]{1,0:T(8,128)(2,1)S(1)}, bf16[64,768]{1,0:T(8,128)(2,1)S(1)}, u32[]{:S(2)}, u32[]{:S(2)}) collective-permute-start(bf16[64,768]{1,0:T(8,128)(2,1)S(1)} %add_convert_fusion.1), channel_id=1, source_target_pairs={{0,16},{8,24},{16,0},{24,8},{1,17},{9,25},{17,1},{25,9},{2,18},{10... | collective-permute-start | bytes 294920 | tf_op jit(solution)/shard_map/ppermute | solution.py:148
  32.0 0.7 %copy-start.1 = (bf16[128,768]{1,0:T(8,128)(2,1)}, bf16[128,768]{1,0:T(8,128)(2,1)S(1)}, u32[]{:S(2)}) copy-start(bf16[128,768]{1,0:T(8,128)(2,1)S(1)} %get-tuple-element.77) | copy-start | bytes 589828
